TPU v7x, 32 devices: a whole 2x2x4 slice. The times are simulated.
32 devices in a mesh: dp: 8 (over z, y), tensor: 4 (over x, core).
Axes of the slice: x: 2, y: 2, z: 4, core: 2. Of those that a mesh axis runs over, the one named last changes fastest.
Arguments:
- enc_input: bfloat16 [8192, 768], P(('dp', 'tensor')), may hold values from -6 to 6
- dec_input: bfloat16 [2048, 768], P(('dp', 'tensor')), may hold values from -6 to 6
- segment_ids: int32 [8, 1024], P('dp'), may hold values from 0 to 7, never falling along the last dimension, each value on 1 to 512 neighbouring positions
- retrieval: int32 [8, 256, 12, 128], P('dp', None, 'tensor'), may hold values from 0 to 1023
- att_in: bfloat16 [9, 768, 768], P(None, None, 'tensor'), may hold values from -0.21875 to 0.21875
- att_in_bias: bfloat16 [6, 768], P(None, 'tensor'), may hold values from -3 to 3
- att_out: bfloat16 [3, 768, 768], P(None, None, 'tensor'), may hold values from -0.875 to 0.875
- att_out_bias: bfloat16 [3, 768], replicated, may hold values from -3 to 3
- ffn_in: bfloat16 [2, 768, 3072], P(None, None, 'tensor'), may hold values from -0.21875 to 0.21875
- ffn_in_bias: bfloat16 [2, 3072], P(None, 'tensor'), may hold values from -3 to 3
- ffn_out: bfloat16 [2, 768, 3072], P(None, None, 'tensor'), may hold values from -0.109375 to 0.109375
- ffn_out_bias: bfloat16 [2, 768], replicated, may hold values from -3 to 3
- ln_gain: bfloat16 [5, 768], replicated, may hold values from 0.5 to 1.5
- ln_bias: bfloat16 [5, 768], replicated, may hold values from -3 to 3
- d_out: bfloat16 [2048, 768], P(('dp', 'tensor')), may hold values from -6 to 6
Outputs:
- dec_output: bfloat16 [2048, 768], P(('dp', 'tensor'))
- enc_input_grad: float32 [8192, 768], P(('dp', 'tensor'))
- dec_input_grad: float32 [2048, 768], P(('dp', 'tensor'))
- att_in_grad: float32 [9, 768, 768], P(None, 'dp', 'tensor')
- att_in_bias_grad: float32 [6, 768], replicated
- att_out_grad: float32 [3, 768, 768], P(None, 'dp', 'tensor')
- att_out_bias_grad: float32 [3, 768], replicated
- ffn_in_grad: float32 [2, 768, 3072], P(None, 'dp', 'tensor')
- ffn_in_bias_grad: float32 [2, 3072], replicated
- ffn_out_grad: float32 [2, 768, 3072], P(None, 'dp', 'tensor')
- ffn_out_bias_grad: float32 [2, 768], replicated
- ln_gain_grad: float32 [5, 768], replicated
- ln_bias_grad: float32 [5, 768], replicated
- rms_values: float32 [7], replicated
Inputs may be any that keep to these rules, and one draw needn't show every extreme that they name: `segment_ids`: along a sequence the ids never fall; every document has 1 to 512 tokens and some document has exactly 512. `retrieval`: each entry is a position among the encoder tokens of the same sequence; entries of one token and head may repeat.
All inputs are finite; a program needn't handle non-finite values.
Results may differ from a plain program's by a relative error of at most 0.025.
Values may be sent and summed in bfloat16 or wider, within the bound.
A program may use at most 192 MiB of HBM per device.

v0:
```python
from functools import partial

import jax
import jax.numpy as jnp
from jax import lax
from jax.sharding import PartitionSpec as P

D = 768
HEAD_DIM = 64
FF = 3072


epsilon = 1e-05


def rounded(value):
    return value.astype(jnp.bfloat16)


def product(left, right):
    return jnp.dot(left, right, preferred_element_type=jnp.float32)


def product_against(left, right):
    return lax.dot_general(
        left, right, (((1,), (1,)), ((), ())), preferred_element_type=jnp.float32
    )


def product_over_rows(left, right):
    return lax.dot_general(
        left, right, (((0,), (0,)), ((), ())), preferred_element_type=jnp.float32
    )


def layer_norm(values, gain, shift):
    center = values - jnp.mean(values, axis=-1, keepdims=True)
    spread = jnp.mean(center * center, axis=-1, keepdims=True)
    return center * lax.rsqrt(spread + epsilon) * gain + shift


def exact_gelu(value):
    return jax.nn.gelu(value, approximate=False)


def rows_gather(block):
    return lax.all_gather(block, "tensor", axis=0, tiled=True)


def grads_gather(block):
    return lax.all_gather(block, "tensor", axis=0, tiled=True)


def rows_reduce(partial_sum):
    return lax.psum_scatter(partial_sum, "tensor", scatter_dimension=0, tiled=True)


def grads_reduce(partial_sum):
    return lax.psum_scatter(partial_sum, "tensor", scatter_dimension=0, tiled=True)


def attend_block(queries, key_rows, values, weights):
    scores = (
        jnp.einsum("qhe,khe->hqk", queries, key_rows, preferred_element_type=jnp.float32) * 0.125
    )
    masked = jnp.where(weights > 0, scores, -1e30)
    top = jnp.max(masked, axis=-1, keepdims=True)
    expo = weights * jnp.exp(scores - top)
    total = jnp.sum(expo, axis=-1, keepdims=True)
    probs = rounded(expo / total)
    mixed = jnp.einsum("hqk,khe->qhe", probs, values, preferred_element_type=jnp.float32)
    return (mixed, top + jnp.log(total))


def attend_back(queries, key_rows, values, weights, logsum, upstream):
    scores = (
        jnp.einsum("qhe,khe->hqk", queries, key_rows, preferred_element_type=jnp.float32) * 0.125
    )
    probs = weights * jnp.exp(scores - logsum)
    dprobs = jnp.einsum("qhe,khe->hqk", upstream, values, preferred_element_type=jnp.float32)
    dscores = rounded(probs * (dprobs - jnp.sum(probs * dprobs, axis=-1, keepdims=True)))
    dquery = (
        jnp.einsum("hqk,khe->qhe", dscores, key_rows, preferred_element_type=jnp.float32) * 0.125
    )
    dkey = jnp.einsum("hqk,qhe->khe", dscores, queries, preferred_element_type=jnp.float32) * 0.125
    dvalue = jnp.einsum(
        "hqk,qhe->khe", rounded(probs), upstream, preferred_element_type=jnp.float32
    )
    return (dquery, dkey, dvalue)


def segment_weights(segments):

    def build(first, start, width, span):
        own = lax.dynamic_slice_in_dim(segments, first, width, 0)
        return (own[:, None] == segments[None, :]).astype(jnp.float32)[None]

    return build


def causal_weights(length):

    def build(first, start, width, span):
        row_index = first + lax.broadcasted_iota(jnp.int32, (width, span), 0)
        col_index = start + lax.broadcasted_iota(jnp.int32, (width, span), 1)
        keep = (row_index // length == col_index // length) & (row_index >= col_index)
        return keep.astype(jnp.float32)[None]

    return build


def blocked_forward(queries, key_rows, values, span, build):
    total = queries.shape[0]
    width = min(512, span)
    count = total // width

    def one_block(index):
        first = index * width
        start = first // span * span
        block_q = lax.dynamic_slice_in_dim(queries, first, width, 0)
        return attend_block(block_q, key_rows, values, build(first, start, width, span))

    mixed, logsum = lax.map(one_block, jnp.arange(count, dtype=jnp.int32))
    return (mixed.reshape(queries.shape), logsum)


def blocked_back(queries, key_rows, values, logsum, upstream, span, build):
    total = queries.shape[0]
    width = min(512, span)
    count = total // width
    groups = total // span

    def one_block(inputs):
        index, block_sum = inputs
        first = index * width
        start = first // span * span
        block_q = lax.dynamic_slice_in_dim(queries, first, width, 0)
        block_up = lax.dynamic_slice_in_dim(upstream, first, width, 0)
        return attend_back(
            block_q, key_rows, values, build(first, start, width, span), block_sum, block_up
        )

    dquery, dkey, dvalue = lax.map(one_block, (jnp.arange(count, dtype=jnp.int32), logsum))
    shape = (groups, count // groups, span, key_rows.shape[1], key_rows.shape[2])
    dkey = jnp.sum(dkey.reshape(shape), axis=1).reshape(key_rows.shape)
    dvalue = jnp.sum(dvalue.reshape(shape), axis=1).reshape(values.shape)
    return (dquery.reshape(queries.shape), dkey, dvalue)


def cross_forward(queries, key_rows, values, counts):
    seqs = counts.shape[0]
    mixed, logsum = jax.vmap(attend_block)(
        queries.reshape(seqs, -1, queries.shape[1], queries.shape[2]),
        key_rows.reshape(seqs, -1, key_rows.shape[1], key_rows.shape[2]),
        values.reshape(seqs, -1, values.shape[1], values.shape[2]),
        counts,
    )
    return (mixed.reshape(queries.shape), logsum)


def cross_back(queries, key_rows, values, logsum, upstream, counts):
    seqs = counts.shape[0]
    dquery, dkey, dvalue = jax.vmap(attend_back)(
        queries.reshape(seqs, -1, queries.shape[1], queries.shape[2]),
        key_rows.reshape(seqs, -1, key_rows.shape[1], key_rows.shape[2]),
        values.reshape(seqs, -1, values.shape[1], values.shape[2]),
        counts,
        logsum,
        upstream.reshape(seqs, -1, upstream.shape[1], upstream.shape[2]),
    )
    return (
        dquery.reshape(queries.shape),
        dkey.reshape(key_rows.shape),
        dvalue.reshape(values.shape),
    )


def retrieval_counts(retrieval, length):
    seqs, steps, heads, picks = retrieval.shape
    width = min(16, steps)
    count = steps // width
    positions = lax.broadcasted_iota(jnp.int32, (1, 1, 1, 1, length), 4)

    def one_block(index):
        block = lax.dynamic_slice_in_dim(retrieval, index * width, width, 1)
        hits = (block[..., None] == positions).astype(jnp.float32)
        return jnp.sum(hits, axis=3)

    blocks = lax.map(one_block, jnp.arange(count, dtype=jnp.int32))
    return jnp.transpose(blocks, (1, 3, 0, 2, 4)).reshape(seqs, heads, steps, length)


def attention_forward(source, memory, index, att_in, att_in_bias, att_out, scorer):
    heads = att_in.shape[2] // HEAD_DIM
    queries = rounded(product(source, att_in[3 * index]) + att_in_bias[2 * index])
    key_rows = rounded(product(memory, att_in[3 * index + 1]))
    values = rounded(product(memory, att_in[3 * index + 2]) + att_in_bias[2 * index + 1])
    queries = queries.reshape(source.shape[0], heads, HEAD_DIM)
    key_rows = key_rows.reshape(memory.shape[0], heads, HEAD_DIM)
    values = values.reshape(memory.shape[0], heads, HEAD_DIM)
    mixed, logsum = scorer(queries, key_rows, values)
    joined = rounded(mixed).reshape(source.shape[0], heads * HEAD_DIM)
    return (product_against(joined, att_out[index]), (queries, key_rows, values, joined, logsum))


def attention_back(source, memory, index, kept, upstream, att_in, att_out, scorer_back):
    queries, key_rows, values, joined, logsum = kept
    dmixed = rounded(product(upstream, att_out[index])).reshape(queries.shape)
    grad_out = product_over_rows(upstream, joined)
    dquery, dkey, dvalue = scorer_back(queries, key_rows, values, logsum, dmixed)
    dquery = rounded(dquery).reshape(source.shape[0], -1)
    dkey = rounded(dkey).reshape(memory.shape[0], -1)
    dvalue = rounded(dvalue).reshape(memory.shape[0], -1)
    grads = (
        product_over_rows(source, dquery),
        product_over_rows(memory, dkey),
        product_over_rows(memory, dvalue),
    )
    biases = (
        jnp.sum(dquery.astype(jnp.float32), axis=0),
        jnp.sum(dvalue.astype(jnp.float32), axis=0),
    )
    dsource = product_against(dquery, att_in[3 * index])
    dmemory = product_against(dkey, att_in[3 * index + 1]) + product_against(
        dvalue, att_in[3 * index + 2]
    )
    return (dsource, dmemory, grads, biases, grad_out)


def feed_forward(source, index, ffn_in, ffn_in_bias, ffn_out):
    before = product(source, ffn_in[index]) + ffn_in_bias[index]
    active = rounded(exact_gelu(before))
    return (product_against(active, ffn_out[index]), (before, active))


def feed_back(source, kept, upstream, index, ffn_in, ffn_out):
    before, active = kept
    dactive = product(upstream, ffn_out[index])
    _, pullback = jax.vjp(exact_gelu, before)
    dbefore = rounded(pullback(dactive)[0])
    grad_out = product_over_rows(upstream, active)
    grad_in = product_over_rows(source, dbefore)
    bias_in = jnp.sum(dbefore.astype(jnp.float32), axis=0)
    return (product_against(dbefore, ffn_in[index]), grad_in, bias_in, grad_out)


def body(
    enc_input,
    dec_input,
    segment_ids,
    retrieval,
    att_in,
    att_in_bias,
    att_out,
    att_out_bias,
    ffn_in,
    ffn_in_bias,
    ffn_out,
    ffn_out_bias,
    ln_gain,
    ln_bias,
    d_out,
):
    length = segment_ids.shape[1]
    steps = retrieval.shape[1]
    dec_rows = segment_ids.shape[0] * steps
    counts = retrieval_counts(retrieval, length)
    enc_scores = partial(
        blocked_forward, span=length, build=segment_weights(segment_ids.reshape(-1))
    )
    enc_grads = partial(blocked_back, span=length, build=segment_weights(segment_ids.reshape(-1)))
    dec_scores = partial(blocked_forward, span=dec_rows, build=causal_weights(steps))
    dec_grads = partial(blocked_back, span=dec_rows, build=causal_weights(steps))
    cross_scores = partial(cross_forward, counts=counts)
    cross_grads = partial(cross_back, counts=counts)
    enc_source = rows_gather(enc_input)
    partial0, kept0 = attention_forward(
        enc_source, enc_source, 0, att_in, att_in_bias, att_out, enc_scores
    )
    branch0 = rows_reduce(partial0) + att_out_bias[0].astype(jnp.float32)
    summed1 = enc_input.astype(jnp.float32) + branch0
    outer1 = layer_norm(summed1, ln_gain[0].astype(jnp.float32), ln_bias[0].astype(jnp.float32))
    hidden_source = rows_gather(rounded(outer1))
    partial1, kept1 = feed_forward(hidden_source, 0, ffn_in, ffn_in_bias, ffn_out)
    branch1 = rows_reduce(partial1) + ffn_out_bias[0].astype(jnp.float32)
    summed2 = outer1 + branch1
    outer2 = layer_norm(summed2, ln_gain[1].astype(jnp.float32), ln_bias[1].astype(jnp.float32))
    memory = rows_gather(rounded(outer2))
    dec_source = rows_gather(dec_input)
    partial2, kept2 = attention_forward(
        dec_source, dec_source, 1, att_in, att_in_bias, att_out, dec_scores
    )
    branch2 = rows_reduce(partial2) + att_out_bias[1].astype(jnp.float32)
    summed3 = dec_input.astype(jnp.float32) + branch2
    outer3 = layer_norm(summed3, ln_gain[2].astype(jnp.float32), ln_bias[2].astype(jnp.float32))
    query_source = rows_gather(rounded(outer3))
    partial3, kept3 = attention_forward(
        query_source, memory, 2, att_in, att_in_bias, att_out, cross_scores
    )
    branch3 = rows_reduce(partial3) + att_out_bias[2].astype(jnp.float32)
    summed4 = outer3 + branch3
    outer4 = layer_norm(summed4, ln_gain[3].astype(jnp.float32), ln_bias[3].astype(jnp.float32))
    feed_source = rows_gather(rounded(outer4))
    partial4, kept4 = feed_forward(feed_source, 1, ffn_in, ffn_in_bias, ffn_out)
    branch4 = rows_reduce(partial4) + ffn_out_bias[1].astype(jnp.float32)
    summed5 = outer4 + branch4
    outer5 = layer_norm(summed5, ln_gain[4].astype(jnp.float32), ln_bias[4].astype(jnp.float32))
    dec_output = rounded(outer5)

    def norm_back(summed, index, upstream):
        _, pullback = jax.vjp(
            layer_norm,
            summed,
            ln_gain[index].astype(jnp.float32),
            ln_bias[index].astype(jnp.float32),
        )
        return pullback(upstream)

    dmix5, gain4, shift4 = norm_back(summed5, 4, d_out.astype(jnp.float32))
    dfeed4, grad_in4, bias_in4, grad_out4 = feed_back(
        feed_source, kept4, grads_gather(rounded(dmix5)), 1, ffn_in, ffn_out
    )
    dmix4, gain3, shift3 = norm_back(summed4, 3, dmix5 + grads_reduce(dfeed4))
    dquery3, dmemory3, proj3, bias3, out3 = attention_back(
        query_source, memory, 2, kept3, grads_gather(rounded(dmix4)), att_in, att_out, cross_grads
    )
    dstream3 = dmix4 + grads_reduce(dquery3)
    dmemory_total = grads_reduce(dmemory3)
    dmix3, gain2, shift2 = norm_back(summed3, 2, dstream3)
    dself2, dmem2, proj2, bias2, out2 = attention_back(
        dec_source, dec_source, 1, kept2, grads_gather(rounded(dmix3)), att_in, att_out, dec_grads
    )
    dec_input_grad = dmix3 + grads_reduce(dself2 + dmem2)
    decoder_parts = (
        jnp.stack(proj2 + proj3),
        jnp.stack((out2, out3)),
        grad_in4[None],
        grad_out4[None],
    )
    dmix2, gain1, shift1 = norm_back(summed2, 1, dmemory_total)
    dfeed1, grad_in1, bias_in1, grad_out1 = feed_back(
        hidden_source, kept1, grads_gather(rounded(dmix2)), 0, ffn_in, ffn_out
    )
    dmix1, gain0, shift0 = norm_back(summed1, 0, dmix2 + grads_reduce(dfeed1))
    dself0, dmem0, proj0, bias0, out0 = attention_back(
        enc_source, enc_source, 0, kept0, grads_gather(rounded(dmix1)), att_in, att_out, enc_grads
    )
    enc_grad = dmix1 + grads_reduce(dself0 + dmem0)
    parts = (jnp.stack(proj0), out0[None], grad_in1[None], grad_out1[None])
    extras = (dmix1, dmix2, gain1, shift1, gain0, shift0, bias_in1, bias0)
    enc_input_grad, encoder_parts, extras = (enc_grad, parts, extras)
    whole = tuple(
        (
            jnp.concatenate((first, second), axis=0)
            for first, second in zip(encoder_parts, decoder_parts)
        )
    )
    summed = lax.psum_scatter(whole, "dp", scatter_dimension=1, tiled=True)
    dmix1, dmix2, gain1, shift1, gain0, shift0, bias_in1, bias0 = extras
    column = lax.axis_index("tensor")
    att_width = att_in.shape[2]
    ffn_width = ffn_in.shape[2]
    att_bias_local = jnp.stack(bias0 + bias2 + bias3)
    ffn_bias_local = jnp.stack((bias_in1, bias_in4))
    wide_att = lax.dynamic_update_slice(
        jnp.zeros((6, D), jnp.float32), att_bias_local, (jnp.int32(0), column * att_width)
    )
    wide_ffn = lax.dynamic_update_slice(
        jnp.zeros((2, FF), jnp.float32), ffn_bias_local, (jnp.int32(0), column * ffn_width)
    )
    out_bias = jnp.stack((jnp.sum(dmix1, axis=0), jnp.sum(dmix3, axis=0), jnp.sum(dmix4, axis=0)))
    ffn_out_bias_part = jnp.stack((jnp.sum(dmix2, axis=0), jnp.sum(dmix5, axis=0)))
    gains = jnp.stack((gain0, gain1, gain2, gain3, gain4))
    shifts = jnp.stack((shift0, shift1, shift2, shift3, shift4))
    squares = jnp.stack(
        (
            jnp.sum(branch0 * branch0),
            jnp.sum(branch1 * branch1),
            jnp.sum(branch2 * branch2),
            jnp.sum(branch3 * branch3),
            jnp.sum(branch4 * branch4),
            jnp.sum(outer2 * outer2),
            jnp.sum(outer5 * outer5),
        )
    )
    totals = lax.psum(
        (wide_att, out_bias, wide_ffn, ffn_out_bias_part, gains, shifts, squares), ("dp", "tensor")
    )
    devices = lax.axis_size("dp") * lax.axis_size("tensor")
    enc_count = 1.0 * enc_input.shape[0] * devices * D
    dec_count = 1.0 * dec_input.shape[0] * devices * D
    number = jnp.array(
        [enc_count, enc_count, dec_count, dec_count, dec_count, enc_count, dec_count],
        dtype=jnp.float32,
    )
    rms_values = jnp.sqrt(totals[6] / number)
    return (
        dec_output,
        enc_input_grad,
        dec_input_grad,
        summed[0],
        totals[0],
        summed[1],
        totals[1],
        summed[2],
        totals[2],
        summed[3],
        totals[3],
        totals[4],
        totals[5],
        rms_values,
    )


def solution(mesh):
    placed = (
        P(("dp", "tensor"), None),
        P(("dp", "tensor"), None),
        P("dp", None),
        P("dp", None, "tensor", None),
        P(None, None, "tensor"),
        P(None, "tensor"),
        P(None, None, "tensor"),
        P(),
        P(None, None, "tensor"),
        P(None, "tensor"),
        P(None, None, "tensor"),
        P(),
        P(),
        P(),
        P(("dp", "tensor"), None),
    )
    return jax.shard_map(
        body,
        mesh=mesh,
        in_specs=placed,
        out_specs=(
            P(("dp", "tensor"), None),
            P(("dp", "tensor"), None),
            P(("dp", "tensor"), None),
            P(None, "dp", "tensor"),
            P(),
            P(None, "dp", "tensor"),
            P(),
            P(None, "dp", "tensor"),
            P(),
            P(None, "dp", "tensor"),
            P(),
            P(),
            P(),
            P(),
        ),
        check_vma=False,
    )
```

profile of v0, /device:TPU:0, one launch (start us, length us, event | category | flops | bytes accessed | tf_op | source)
XLA Modules:
  0.0 1208.5 jit_solution(2214733194497263711)
XLA Ops:
  9.5 22.5 %all-gather.6.cloned.1.call-done = bf16[1024,768]{1,0:T(8,128)(2,1)} async-done(((bf16[256,768]{1,0:T(8,128)(2,1)}), bf16[1024,768]{1,0:T(8,128)(2,1)}) %all-gather.6.cloned.1.call-update) | async-done | bytes 1572880 | tf_op jit(solution)/shard_map/all_gather | solution.py:47
  38.0 14.3 %while.11 = (s32[]{:T(128)}, bf16[2,512,3,64]{1,3,2,0:T(8,128)(2,1)S(1)}, f32[2,3,512,1]{2,1,3,0:T(4,128)S(1)}, s32[2]{0:T(128)S(1)}, s32[1024]{0:T(1024)S(1)}, ...) while((s32[]{:T(128)}, ...), condition=%wide.region_8.9_spmd, body=%wide.region_5.8_spmd.sunk | while | flops 423098880 | bytes 27660488 | solution.py:123
  57.3 36.7 %reduce-scatter.22.cloned.1.call-done = f32[256,768]{1,0:T(8,128)} async-done(((f32[1024,768]{1,0:T(8,128)}), f32[256,768]{1,0:T(8,128)}) %reduce-scatter.22.cloned.1.call-update) | async-done | bytes 786448 | tf_op jit(solution)/shard_map/reduce_scatter | solution.py:55
  97.9 19.1 %all-gather.8.cloned.1.call-done = bf16[1024,768]{1,0:T(8,128)(2,1)} async-done(((bf16[256,768]{1,0:T(8,128)(2,1)}), bf16[1024,768]{1,0:T(8,128)(2,1)}) %all-gather.8.cloned.1.call-update) | async-done | bytes 1572880 | tf_op jit(solution)/shard_map/all_gather | solution.py:47
  117.0 11.5 multiply_convert_fusion.2
  147.5 23.7 %reduce-scatter.24.cloned.1.call-done = f32[256,768]{1,0:T(8,128)} async-done(((f32[1024,768]{1,0:T(8,128)}), f32[256,768]{1,0:T(8,128)}) %reduce-scatter.24.cloned.1.call-update) | async-done | bytes 786448 | tf_op jit(solution)/shard_map/reduce_scatter | solution.py:55
  175.3 131.8 %while.13 = (s32[]{:T(128)}, f32[16,1,16,3,1024]{4,3,2,1,0:T(4,128)}, s32[16]{0:T(128)S(1)}, s32[1,256,3,128]{3,1,2,0:T(8,128)}, s32[]{:T(128)}, /*index=5*/s32[1]{0:T(128)}, s32[]{:T(128)}, s32[]{:T(128)}) while((s32[]{:T(128)}, f32[16,1,16,3,1024]{4,3,2,1,0:T(4,128)}, s32[16]{0:T(128)S(1)}, s32[1,256,3,128]{3,1,2,0:T(8,128)}, ...), condition=%wide.region_17.18_spmd.clone, body=%wide.region_15.17_spmd.clone.sunk | while | flops 18825220 | bytes 778899 | solution.py:189
  335.2 23.7 %reduce-scatter.26.cloned.1.call-done = f32[64,768]{1,0:T(8,128)} async-done(((f32[256,768]{1,0:T(8,128)}), f32[64,768]{1,0:T(8,128)}) %reduce-scatter.26.cloned.1.call-update) | async-done | bytes 196624 | tf_op jit(solution)/shard_map/reduce_scatter | solution.py:55
  375.6 23.7 %reduce-scatter.28.cloned.1.call-done = f32[64,768]{1,0:T(8,128)} async-done(((f32[256,768]{1,0:T(8,128)}), f32[64,768]{1,0:T(8,128)}) %reduce-scatter.28.cloned.1.call-update) | async-done | bytes 196624 | tf_op jit(solution)/shard_map/reduce_scatter | solution.py:55
  419.6 22.4 %reduce-scatter.30.cloned.1.call-done = f32[64,768]{1,0:T(8,128)} async-done(((f32[256,768]{1,0:T(8,128)}), f32[64,768]{1,0:T(8,128)}) %reduce-scatter.30.cloned.1.call-update) | async-done | bytes 196624 | tf_op jit(solution)/shard_map/reduce_scatter | solution.py:59
  465.2 38.3 %reduce-scatter.32.cloned.1.call-done = f32[256,768]{1,0:T(8,128)} async-done(((f32[1024,768]{1,0:T(8,128)}), f32[256,768]{1,0:T(8,128)}) %reduce-scatter.32.cloned.1.call-update) | async-done | bytes 786448 | tf_op jit(solution)/shard_map/reduce_scatter | solution.py:59
  512.5 15.7 %all-gather.12.cloned.1.call-done = bf16[1024,768]{1,0:T(8,128)(2,1)} async-done(((bf16[256,768]{1,0:T(8,128)(2,1)}), bf16[1024,768]{1,0:T(8,128)(2,1)}) %all-gather.12.cloned.1.call-update) | async-done | bytes 1572880 | tf_op jit(solution)/shard_map/all_gather | solution.py:51
  528.1 6.6 convert_reduce_fusion.1
  546.1 8.4 reduce-scatter.38.cloned.1.call-done
  564.0 31.1 %reduce-scatter.34.cloned.1.call-done = f32[256,768]{1,0:T(8,128)} async-done(((f32[1024,768]{1,0:T(8,128)}), f32[256,768]{1,0:T(8,128)}) %reduce-scatter.34.cloned.1.call-update) | async-done | bytes 786448 | tf_op jit(solution)/shard_map/reduce_scatter | solution.py:59
  621.6 21.8 %while.12 = (s32[]{:T(128)}, bf16[2,512,3,64]{1,3,2,0:T(8,128)(2,1)S(1)}, f32[2,1024,3,64]{1,3,2,0:T(8,128)}, f32[2,1024,3,64]{1,3,2,0:T(8,128)}, s32[2]{0:T(128...) while((s32[]{:T(128)}, ...), condition=%wide.region_40.41_spmd, body=%wide.region_38.40_spmd.sunk | while | flops 1031567872 | bytes 72147752 | solution.py:143
  676.1 12.3 %copy.71 = f32[9,768,192]{2,0,1:T(8,128)} copy(f32[9,768,192]{1,2,0:T(8,128)} %fusion.44) | data formatting | bytes 10616832
  688.3 10.2 reshape.813
  715.1 63.4 %all-reduce.3.cloned.1.call-done = (f32[6,768]{1,0:T(8,128)}, f32[3,768]{1,0:T(4,128)}, f32[2,3072]{1,0:T(2,128)}, f32[2,768]{1,0:T(2,128)}, f32[5,768]{1,0:T(8,128)}, /*index=5*/f32[5,768]{1,0:T(8,128)}, f32[7]{0:T(128)}) async-done(((f32[6,768]{1,0:T(8,128)}, f32[3,768]{1,0:T(4,128)}, f32[2,3072]{1,0:T(2,128)}, f32[2,768]{1,0:T(2,128)}, f32[5,768]{1,0:T(8,128)}, /*index=5*/f32[5,768]{1,0:T(8,128)}, ...) | async-done | bytes 89132 | tf_op jit(solution)/shard_map/psum | solution.py:386
  779.7 69.2 %reduce-scatter.48.cloned.1.call-done = f32[96,576]{1,0:T(8,128)} async-done(((f32[768,576]{1,0:T(8,128)}), f32[96,576]{1,0:T(8,128)}) %reduce-scatter.48.cloned.1.call-update) | async-done | bytes 221200
  850.8 37.4 %reduce-scatter.36.cloned.1.call-done = f32[256,768]{1,0:T(8,128)} async-done(((f32[1024,768]{1,0:T(8,128)}), f32[256,768]{1,0:T(8,128)}) %reduce-scatter.36.cloned.1.call-update) | async-done | bytes 786448 | tf_op jit(solution)/shard_map/reduce_scatter | solution.py:59
  890.3 108.2 %reduce-scatter.46.cloned.1.call-done = f32[96,1728]{1,0:T(8,128)} async-done(((f32[768,1728]{1,0:T(8,128)}), f32[96,1728]{1,0:T(8,128)}) %reduce-scatter.46.cloned.1.call-update) | async-done | bytes 663568
  1001.5 96.7 %reduce-scatter.44.cloned.1.call-done = f32[2,96,768]{2,1,0:T(8,128)} async-done(((f32[2,768,768]{2,1,0:T(8,128)}), f32[2,96,768]{2,1,0:T(8,128)}) %reduce-scatter.44.cloned.1.call-update) | async-done | bytes 589840 | tf_op jit(solution)/shard_map/reduce_scatter | solution.py:358
  1098.2 99.4 %reduce-scatter.42.cloned.1.call-done = f32[2,96,768]{2,1,0:T(8,128)} async-done(((f32[2,768,768]{2,1,0:T(8,128)}), f32[2,96,768]{2,1,0:T(8,128)}) %reduce-scatter.42.cloned.1.call-update) | async-done | bytes 589840 | tf_op jit(solution)/shard_map/reduce_scatter | solution.py:358
  (698 shorter events, 397.5 us)
Async XLA Ops:
  7.2 24.8 %all-gather.6.cloned.1.call-start = ((), (), s32[]{:S(2)}) async-start(), calls=%async_computation.16 | async-start | bytes 1966080 | tf_op jit(solution)/shard_map/all_gather | solution.py:47
  7.9 86.1 %reduce-scatter.22.cloned.1.call-start = ((), (), s32[]{:S(2)}) async-start(), calls=%async_computation.17 | async-start | bytes 3932160 | tf_op jit(solution)/shard_map/reduce_scatter | solution.py:55
  55.9 61.1 %all-gather.8.cloned.1.call-start = ((), (), s32[]{:S(2)}) async-start(), calls=%async_computation.18 | async-start | bytes 1966080 | tf_op jit(solution)/shard_map/all_gather | solution.py:47
  97.2 73.9 %reduce-scatter.24.cloned.1.call-start = ((), (), s32[]{:S(2)}) async-start(), calls=%async_computation.19 | async-start | bytes 3932160 | tf_op jit(solution)/shard_map/reduce_scatter | solution.py:55
  133.0 178.1 %reduce-scatter.20.cloned.1.call-start = ((), (), s32[]{:S(2)}) async-start(), calls=%async_computation.15 | async-start | bytes 983040 | tf_op jit(solution)/shard_map/reduce_scatter | solution.py:55
  146.8 176.4 %all-gather.10.cloned.1.call-start = ((), (), s32[]{:S(2)}) async-start(), calls=%async_computation.20 | async-start | bytes 1966080 | tf_op jit(solution)/shard_map/all_gather | solution.py:47
  175.2 183.6 %reduce-scatter.26.cloned.1.call-start = ((), (), s32[]{:S(2)}) async-start(), calls=%async_computation.21 | async-start | bytes 983040 | tf_op jit(solution)/shard_map/reduce_scatter | solution.py:55
  335.1 64.1 %reduce-scatter.28.cloned.1.call-start = ((), (), s32[]{:S(2)}) async-start(), calls=%async_computation.22 | async-start | bytes 983040 | tf_op jit(solution)/shard_map/reduce_scatter | solution.py:55
  375.5 66.5 %reduce-scatter.30.cloned.1.call-start = ((), (), s32[]{:S(2)}) async-start(), calls=%async_computation.23 | async-start | bytes 983040 | tf_op jit(solution)/shard_map/reduce_scatter | solution.py:59
  418.3 85.3 %reduce-scatter.32.cloned.1.call-start = ((), (), s32[]{:S(2)}) async-start(), calls=%async_computation.24 | async-start | bytes 3932160 | tf_op jit(solution)/shard_map/reduce_scatter | solution.py:59
  465.1 63.0 %all-gather.12.cloned.1.call-start = ((), (), s32[]{:S(2)}) async-start(), calls=%async_computation.25 | async-start | bytes 1966080 | tf_op jit(solution)/shard_map/all_gather | solution.py:51
  508.3 46.2 %reduce-scatter.38.cloned.1.call-start = ((), (), s32[]{:S(2)}) async-start(), calls=%async_computation.29 | async-start | bytes 983040 | tf_op jit(solution)/shard_map/reduce_scatter | solution.py:59
  512.2 82.9 %reduce-scatter.34.cloned.1.call-start = ((), (), s32[]{:S(2)}) async-start(), calls=%async_computation.26 | async-start | bytes 3932160 | tf_op jit(solution)/shard_map/reduce_scatter | solution.py:59
  539.2 80.2 %all-gather.14.cloned.1.call-start = ((), (), s32[]{:S(2)}) async-start(), calls=%async_computation.27 | async-start | bytes 1966080 | tf_op jit(solution)/shard_map/all_gather | solution.py:51
  599.5 113.0 %reduce-scatter.40.cloned.1.call-start = ((), (), s32[]{:S(2)}) async-start(), calls=%async_computation.30 | async-start | bytes 983040 | tf_op jit(solution)/shard_map/reduce_scatter | solution.py:59
  607.8 170.7 %all-reduce.3.cloned.1.call-start = ((), (), s32[]{:S(2)}) async-start(), calls=%async_computation.35 | async-start | bytes 234496 | tf_op jit(solution)/shard_map/psum | solution.py:386
  646.5 202.4 %reduce-scatter.48.cloned.1.call-start = ((), (), s32[]{:S(2)}) async-start(), calls=%async_computation.34 | async-start | bytes 2211840
  655.6 232.6 %reduce-scatter.36.cloned.1.call-start = ((), (), s32[]{:S(2)}) async-start(), calls=%async_computation.28 | async-start | bytes 3932160 | tf_op jit(solution)/shard_map/reduce_scatter | solution.py:59
  663.8 334.8 %reduce-scatter.46.cloned.1.call-start = ((), (), s32[]{:S(2)}) async-start(), calls=%async_computation.33 | async-start | bytes 6193152
  698.5 399.7 %reduce-scatter.44.cloned.1.call-start = ((), (), s32[]{:S(2)}) async-start(), calls=%async_computation.32 | async-start | bytes 5308416 | tf_op jit(solution)/shard_map/reduce_scatter | solution.py:358
  705.5 492.1 %reduce-scatter.42.cloned.1.call-start = ((), (), s32[]{:S(2)}) async-start(), calls=%async_computation.31 | async-start | bytes 5308416 | tf_op jit(solution)/shard_map/reduce_scatter | solution.py:358
  850.8 348.6 %copy-start.148 = (f32[2,768]{1,0:T(2,128)S(1)}, f32[2,768]{1,0:T(2,128)}, u32[]{:S(2)}) copy-start(f32[2,768]{1,0:T(2,128)} %get-tuple-element.734) | copy-start | bytes 18436
  850.8 349.2 %copy-start.102 = (f32[5,768]{1,0:T(8,128)S(1)}, f32[5,768]{1,0:T(8,128)}, u32[]{:S(2)}) copy-start(f32[5,768]{1,0:T(8,128)} %get-tuple-element.735) | copy-start | bytes 46084
  850.8 349.8 %copy-start.101 = (f32[5,768]{1,0:T(8,128)S(1)}, f32[5,768]{1,0:T(8,128)}, u32[]{:S(2)}) copy-start(f32[5,768]{1,0:T(8,128)} %get-tuple-element.736) | copy-start | bytes 46084
  (168 other events, 3442.7 us)
Sparse Core Ops, SparseCore 0:
  9.6 22.3 all-gather.5
  56.0 37.9 reduce-scatter.21
  97.4 19.6 all-gather.7
  133.2 37.9 reduce-scatter.23
  174.1 23.2 reduce-scatter.19
  199.5 19.6 all-gather.9
  335.3 23.5 reduce-scatter.25
  375.6 23.5 reduce-scatter.27
  418.4 23.5 reduce-scatter.29
  465.3 38.2 reduce-scatter.31
  508.4 19.6 all-gather.11
  531.2 23.2 reduce-scatter.37
  557.1 38.0 reduce-scatter.33
  599.6 19.6 all-gather.13
  622.5 23.2 reduce-scatter.39
  653.2 125.2 all-reduce.2
  782.2 66.6 reduce-scatter.47
  851.3 36.8 reduce-scatter.35
  892.2 106.2 reduce-scatter.45
  1002.6 95.5 reduce-scatter.43
  1102.4 95.1 reduce-scatter.41
where the time goes:
time: 1220 us; the launch traced here: 1210 us
  waiting for transfers between devices  744 us (61%)
  other arithmetic  148 us (12%)
  matrix products  132 us (11%)
  local copies, waits for them, and re-layouts  114 us (9%)
  blocking collectives  37.6 us (3%)
  between operations  16.7 us (1%)
  loops' own time  14.2 us (1%)
    reduce_scatter x2, waiting for transfers between devices, body(): summed = lax.psum_scatter(whole, 'dp', scatter_dimension=1, tiled=True)  196 us
    unnamed x23, waiting for transfers between devices  178 us
    reduce_scatter x6, waiting for transfers between devices, grads_reduce(): lax.psum_scatter(partial_sum, 'tensor', scatter_dimension=0, tiled=True)  138 us
    reduce_scatter x5, waiting for transfers between devices, rows_reduce(): lax.psum_scatter(partial_sum, 'tensor', scatter_dimension=0, tiled=True)  108 us
    reduce_sum x16, other arithmetic, one_block(): return jnp.sum(hits, axis=3)  85.3 us
    psum x1, waiting for transfers between devices, body(): lax.psum((wide_att, out_bias, wide_ffn, ffn_out_bias_part, gains, shifts,...  63.4 us
    unnamed x350, local copies, waits for them, and re-layouts  56 us
    dot_general x16, matrix products, product(): return jnp.dot(left, right, preferred_element_type=jnp.float32)  46 us
  transfers between devices with their start and end apart: 21, of which 18 were waited for; matrix products, arithmetic and copies ran while one was open for 23% of the time, Pallas kernels for 0%

commit v1 on v0

v1 whole, which is shorter than its diff:
```python
import functools
from types import SimpleNamespace
from typing import Any, NamedTuple

import jax
import jax.numpy as jnp
from jax import lax
from jax.experimental import pallas as pl
from jax.experimental.pallas import tpu as pltpu
from jax.sharding import PartitionSpec as P

HEAD = 64
EPS = 1e-05
NEG = -1e30
MESH = pl.DeviceIdType.MESH
DP, TENSOR = "dp", "tensor"
PROBS, ALL_GRADS = "probs", "grads"
F32 = jnp.float32
BF16 = jnp.bfloat16

ROW_ATT_OUT_BIAS = 0
ROW_FFN_OUT_BIAS = 3
ROW_GAIN = 5
ROW_SHIFT = 10
ROW_SQUARE = 15
ROW_FFN_IN_BIAS = 24
SUM_ROWS = 32
BIAS_ROWS = 8

ATT, FFN_IN, FFN_OUT = range(3)
GRADS = (
    (FFN_OUT, 1, (1, 2, 4)),
    (FFN_IN, 1, (2, 1, 4)),
    (ATT, 2, (1, 2, 4)),
    (ATT, 1, (2, 1, 4)),
    (FFN_OUT, 0, (1, 2, 4)),
    (FFN_IN, 0, (2, 1, 4)),
    (ATT, 0, (2, 1, 4)),
)
SLOTS = 4


def mm(left, right):
    return jnp.dot(left, right, preferred_element_type=F32)


def mm_nt(left, right):
    return lax.dot_general(left, right, (((1,), (1,)), ((), ())), preferred_element_type=F32)


def mm_tn(left, right):
    return lax.dot_general(left, right, (((0,), (0,)), ((), ())), preferred_element_type=F32)


def bit_of(value, bit):
    return lax.rem(lax.div(value, jnp.int32(bit)), jnp.int32(2))


def flipped(value, bit):
    return value + bit - 2 * bit * bit_of(value, bit)


def column_sum(values):
    return jnp.sum(values, axis=0, keepdims=True)


class Inputs(NamedTuple):
    enc_input: Any
    dec_input: Any
    segment_ids: Any
    retrieval: Any
    att_in: Any
    att_in_bias: Any
    att_out: Any
    att_out_bias: Any
    ffn_in: Any
    ffn_in_bias: Any
    ffn_out: Any
    ffn_out_bias: Any
    ln_gain: Any
    ln_bias: Any
    d_out: Any


IN_HBM = Inputs(
    enc_input=True,
    dec_input=True,
    segment_ids=False,
    retrieval=True,
    att_in=True,
    att_in_bias=False,
    att_out=True,
    att_out_bias=False,
    ffn_in=True,
    ffn_in_bias=False,
    ffn_out=True,
    ffn_out_bias=False,
    ln_gain=False,
    ln_bias=False,
    d_out=True,
)


class Plan:
    def __init__(self, args, n_dp):
        self.D = D = args.enc_input.shape[1]
        self.CE = CE = args.enc_input.shape[0]
        self.HD = HD = args.dec_input.shape[0]
        self.HE = HE = CE // 2
        self.CD = 2 * HD
        self.R = R = 4 * CE
        self.S = S = 4 * HD
        self.A = A = args.att_in.shape[1]
        self.heads = heads = A // HEAD
        self.F = F = args.ffn_in.shape[2]
        self.picks = args.retrieval.shape[3]
        self.inside = n_dp == 8
        self.block = D // 8
        self.scratch = {}
        self.n_sems = 0
        self.at = SimpleNamespace()

        wide = ((R, D), BF16)
        short = ((S, D), BF16)
        enc_heads = ((R, A), BF16)
        dec_heads = ((S, A), BF16)
        enc_float = ((4, HE, D), F32)
        dec_float = ((2, HD, D), F32)
        enc_half = ((4, HE, D), BF16)
        dec_half = ((2, HD, D), BF16)
        enc_column = ((4, HE, 1), F32)
        dec_column = ((2, HD, 1), F32)
        stacked = ((heads * CE, A), BF16)
        self.vmem(
            ATI=((9, A, D), BF16),
            ATO=((3, A, D), BF16),
            FFI=((D, F), BF16),
            FFO=((D, F), BF16),
            RET=((heads, S, self.picks), jnp.int32),
        )
        self.vmem(X=wide, H1=wide, MEM=wide, E2=wide)
        self.vmem(DX=short, G1=short, G2=short, E5=short, E4=short, E3=short)
        self.vmem(DOU=dec_half, G3S=dec_half)
        self.vmem(Q=enc_heads, K=enc_heads, V=enc_heads, O=enc_heads, UP=enc_heads)
        self.vmem(K2=enc_heads, V2=enc_heads)
        self.vmem(QD=dec_heads, KD=dec_heads, VD=dec_heads, OD=dec_heads, UPD=dec_heads)
        self.vmem(Q2=dec_heads, O2=dec_heads, D2=dec_heads)
        self.vmem(DK=((R, A), F32), DV=((R, A), F32))
        self.vmem(BIG=((3, heads * CE, R), BF16), PD=((heads * S, S), BF16), QS=stacked, DOS=stacked)
        self.vmem(ACT0=((R, F), BF16), GP0=((R, F), BF16), ACT1=((S, F), BF16), GP1=((S, F), BF16))
        self.vmem(XH0=enc_float, XH1=enc_float, RES=enc_float)
        self.vmem(XH2=dec_float, XH3=dec_float, XH4=dec_float, RESD=dec_float)
        self.vmem(RS0=enc_column, RS1=enc_column, RS2=dec_column, RS3=dec_column, RS4=dec_column)
        self.vmem(SEGR=((1, R), F32), SEGC=((R, 1), F32), T=((D, R), BF16))
        self.vmem(OWN=((HE, D), F32), OWND=((HD, D), F32))
        self.vmem(PR=enc_half, PS=enc_half, XS=enc_half, XR=((2, 4, HE, D), BF16))
        self.vmem(PRD=dec_half, PSD=dec_half, XSD=dec_half, XRD=((2, 2, HD, D), BF16))
        self.vmem(GR=((SLOTS, 8, self.block, D), BF16))
        if self.inside:
            self.vmem(
                R1=((SLOTS, 4, self.block, D), BF16),
                R2=((SLOTS, 2, self.block, D), BF16),
                R3=((SLOTS, 1, self.block, D), BF16),
                SUMR=((5, SUM_ROWS, D), F32),
                BIAR=((5, 4 * BIAS_ROWS, 256), F32),
            )
        self.vmem(SUM=((SUM_ROWS, D), F32), BIA=((4 * BIAS_ROWS, 256), F32))
        self.vmem(GAIN=((5, D), F32), SHIFT=((5, D), F32))
        self.vmem(AIB=((6, A), F32), AOB=((3, D), F32), FIB=((2, F), F32), FOB=((2, D), F32))
        self.sem(load=8, own=4, ag=24, pst=2, enc=24, dec=12)
        self.sem(H1=8, MEM=8, E2=8, E1=8, G1=4, G2=4, E5=4, E4=4, E3=4)
        self.sem(grad=42, sum=20)

    def vmem(self, **buffers):
        for name, (shape, dtype) in buffers.items():
            self.scratch[name] = pltpu.VMEM(shape, dtype)

    def sem(self, **counts):
        for name, count in counts.items():
            setattr(self.at, name, self.n_sems)
            self.n_sems += count


class Outputs(NamedTuple):
    dec_output: Any
    enc_grad: Any
    dec_grad: Any
    sums: Any
    biases: Any
    probs: Any
    grads: Any = None
    att_in: Any = None
    att_out: Any = None
    ffn_in: Any = None
    ffn_out: Any = None


def kernel(p, made, *refs):
    n_in = len(Inputs._fields)
    ins = Inputs(*refs[:n_in])
    outs = Outputs(*[None if index is None else refs[n_in + index] for index in made])
    n_out = sum(index is not None for index in made)
    b = SimpleNamespace(**dict(zip(p.scratch, refs[n_in + n_out : -2])))
    sems, free = refs[-2:]
    b.CNT, b.DS = b.BIG.at[1], b.BIG.at[2]
    D, A, F, R, S, CE, HE, CD, HD = p.D, p.A, p.F, p.R, p.S, p.CE, p.HE, p.CD, p.HD
    heads, at = p.heads, p.at

    t = lax.axis_index(TENSOR)
    dp = lax.axis_index(DP)
    x, c = lax.div(t, jnp.int32(2)), lax.rem(t, jnp.int32(2))
    pair = (dp, t + 1 - 2 * c)
    across = (dp, t + 2 - 4 * x)

    def sem(base, index):
        return sems.at[base + index]

    def remote(src, dst, base, index, target):
        return pltpu.make_async_remote_copy(
            src_ref=src,
            dst_ref=dst,
            send_sem=sem(base, 2 * index),
            recv_sem=sem(base, 2 * index + 1),
            device_id=target,
            device_id_type=MESH,
        )

    partners = [pair, across]
    if p.inside:
        partners += [(flipped(dp, bit), t) for bit in (1, 2, 4)]
    barrier = pltpu.get_barrier_semaphore()
    for partner in partners:
        pl.semaphore_signal(barrier, inc=1, device_id=partner, device_id_type=MESH)

    loads = [
        pltpu.make_async_copy(ins.retrieval.at[0], b.RET, sem(at.load, 0)),
        pltpu.make_async_copy(ins.att_in, b.ATI, sem(at.load, 1)),
        pltpu.make_async_copy(ins.att_out, b.ATO, sem(at.load, 2)),
    ]
    for copy in loads:
        copy.start()

    def load_ffn(f):
        return (
            pltpu.make_async_copy(ins.ffn_in.at[f], b.FFI, sem(at.load, 3)),
            pltpu.make_async_copy(ins.ffn_out.at[f], b.FFO, sem(at.load, 4)),
        )

    for copy in load_ffn(0):
        copy.start()

    pl.semaphore_wait(barrier, len(partners))

    def place(owner_x, owner_c, half):
        return pl.ds(pl.multiple_of((2 * owner_x + half) * CE + owner_c * HE, HE), HE)

    def enc_copy(half, target, index):
        src = ins.enc_input.at[pl.ds(half * HE, HE)]
        return remote(src, b.X.at[place(x, c, half)], at.ag, index, target)

    def enc_forward(half, index):
        rows = place(1 - x, c, half)
        return remote(b.X.at[rows], b.X.at[rows], at.ag, index, pair)

    dec_rows = pl.ds(pl.multiple_of(t * HD, HD), HD)
    far_rows = pl.ds(pl.multiple_of((t + 2 - 4 * x) * HD, HD), HD)

    def dec_copy(target, index):
        return remote(ins.dec_input, b.DX.at[dec_rows], at.ag, index, target)

    def dec_forward(index):
        return remote(b.DX.at[far_rows], b.DX.at[far_rows], at.ag, index, pair)

    ag_x = [enc_copy(0, across, 0), enc_copy(1, across, 1), dec_copy(across, 2)]
    ag_x.append(remote(ins.d_out, b.DOU.at[x], at.ag, 3, across))
    ag_p = [enc_copy(0, pair, 4), enc_copy(1, pair, 5), dec_copy(pair, 6)]
    ag_f = [enc_forward(0, 7), enc_forward(1, 8), dec_forward(9)]
    for copy in ag_x + ag_p:
        copy.start()
    own_copies = [
        pltpu.make_async_copy(
            ins.enc_input.at[pl.ds(0, HE)], b.X.at[place(x, c, 0)], sem(at.own, 0)
        ),
        pltpu.make_async_copy(
            ins.enc_input.at[pl.ds(HE, HE)], b.X.at[place(x, c, 1)], sem(at.own, 1)
        ),
        pltpu.make_async_copy(ins.dec_input, b.DX.at[dec_rows], sem(at.own, 2)),
        pltpu.make_async_copy(ins.d_out, b.DOU.at[x], sem(at.own, 3)),
    ]
    for copy in own_copies:
        copy.start()

    b.GAIN[...] = ins.ln_gain[...].astype(F32)
    b.SHIFT[...] = ins.ln_bias[...].astype(F32)
    b.AIB[...] = ins.att_in_bias[...].astype(F32)
    b.AOB[...] = ins.att_out_bias[...].astype(F32)
    b.FIB[...] = ins.ffn_in_bias[...].astype(F32)
    b.FOB[...] = ins.ffn_out_bias[...].astype(F32)
    b.SUM[...] = jnp.zeros((SUM_ROWS, D), F32)
    b.BIA[...] = jnp.zeros((4 * BIAS_ROWS, 256), F32)
    segments = ins.segment_ids[...].astype(F32)
    order = (0, 2, 1, 3, 4, 6, 5, 7)
    pieces = [segments[:, HE * o : HE * (o + 1)] for o in order]
    b.SEGR[...] = jnp.concatenate(pieces, axis=1)
    standing = jnp.concatenate(pieces, axis=0).T
    for k in range(8):
        b.SEGC[HE * k : HE * (k + 1), :] = standing[:, k : k + 1]

    lane_head = lax.broadcasted_iota(jnp.int32, (1, A), 1) // HEAD
    head_masks = [lane_head == h for h in range(heads)]
    zero16 = jnp.zeros((), BF16)

    def only_head(values, h):
        return jnp.where(head_masks[h], values, zero16)

    loads[0].wait()
    lanes = p.picks

    def count_block(index, carry):
        base = pl.multiple_of(index * 16, 16)
        for h in range(heads):
            halves = []
            for part in range(2):
                picks = b.RET[h, pl.ds(base + 8 * part, 8), :]
                high = lax.shift_right_logical(picks, 7)
                low = picks & 127
                swapped = (high & 4) | ((high & 1) << 1) | ((high >> 1) & 1)
                code = swapped * 8 + lax.broadcasted_iota(jnp.int32, (8, lanes), 0)
                codes = lax.broadcasted_iota(jnp.int32, (64, lanes), 0)
                lows = lax.broadcasted_iota(jnp.int32, (128, lanes), 0)
                left = jnp.concatenate(
                    [jnp.where(codes == code[k : k + 1, :], 1.0, 0.0).astype(BF16) for k in range(8)],
                    axis=1,
                )
                right = jnp.concatenate(
                    [jnp.where(lows == low[k : k + 1, :], 1.0, 0.0).astype(BF16) for k in range(8)],
                    axis=1,
                )
                halves.append(mm_nt(left, right))
            for k in range(8):
                value = jnp.concatenate([half[8 * k : 8 * k + 8] for half in halves], axis=0)
                b.CNT[pl.ds(h * S + base, 16), 128 * k : 128 * (k + 1)] = value.astype(BF16)
        return carry

    half_count = S // 32
    lax.fori_loop(0, half_count, count_block, 0)
    ag_x[0].wait_recv()
    ag_f[0].start()
    lax.fori_loop(half_count, 2 * half_count, count_block, 0)
    ag_x[1].wait_recv()
    ag_f[1].start()
    ag_x[2].wait_recv()
    ag_f[2].start()
    for copy in own_copies[:3]:
        copy.wait()
    for copy in ag_p:
        copy.wait_recv()
    loads[1].wait()
    loads[2].wait()
    for copy in ag_f:
        copy.wait_recv()

    def project(source, rows, index, target_q, target_k, target_v):
        if target_q is not None:
            bias = b.AIB[2 * index : 2 * index + 1, :]
            value = (mm_nt(source, b.ATI[3 * index]) + bias).astype(BF16)
            target_q[rows, :] = value * jnp.asarray(0.125, BF16)
        if target_k is not None:
            target_k[rows, :] = mm_nt(source, b.ATI[3 * index + 1]).astype(BF16)
            bias = b.AIB[2 * index + 1 : 2 * index + 2, :]
            target_v[rows, :] = (mm_nt(source, b.ATI[3 * index + 2]) + bias).astype(BF16)

    def enc_rows(i):
        return pl.ds(pl.multiple_of(i * CE, CE), CE)

    def dec_chunk(i):
        return pl.ds(pl.multiple_of(i * CD, CD), CD)

    def enc_mine(i):
        return pl.ds(pl.multiple_of(i * CE + c * HE, HE), HE)

    def dec_mine(i):
        return pl.ds(pl.multiple_of(i * CD + c * HD, HD), HD)

    def enc_sum(k):
        s = k % 2

        def pair_copy(i):
            return remote(b.PS.at[i], b.PR.at[i], at.enc, i, pair)

        def across_copy(i):
            return remote(b.XS.at[i], b.XR.at[s, i], at.enc, 4 + 4 * s + i, across)

        return (pair_copy, across_copy, b.OWN, b.PS, b.XS, b.PR, b.XR.at[s], HE)

    def dec_sum(k):
        s = k % 2

        def pair_copy(i):
            return remote(b.PSD.at[i], b.PRD.at[i], at.dec, i, pair)

        def across_copy(i):
            return remote(b.XSD.at[i], b.XRD.at[s, i], at.dec, 2 + 2 * s + i, across)

        return (
            pair_copy,
            across_copy,
            b.OWND,
            b.PSD,
            b.XSD,
            b.PRD,
            b.XRD.at[s],
            HD,
        )

    def pair_send(group, i, part):
        pair_copy, _, own, sent, _, _, _, half = group
        first, second = part[:half], part[half:]
        own[...] = jnp.where(c == 0, first, second)
        sent[i] = jnp.where(c == 0, second, first).astype(BF16)
        pair_copy(i).start()

    def pair_take(group, i):
        pair_copy, _, own, _, _, got, _, _ = group
        copy = pair_copy(i)
        copy.wait()
        return own[...] + got[i].astype(F32)

    def across_send(group, i):
        _, across_copy, _, _, sent, _, _, _ = group
        sent[i] = pair_take(group, i).astype(BF16)
        across_copy(i).start()

    def across_take(group, i):
        _, across_copy, _, _, sent, _, got, _ = group
        across_copy(i).wait()
        return sent[i].astype(F32) + got[i].astype(F32)

    def gather_copy(base, target, rows, i):
        return remote(target.at[rows], target.at[rows], base, i, pair)

    def gather_start(base, target, rows, i, value):
        target[rows, :] = value
        gather_copy(base, target, rows, i).start()

    def norm(index, value, xhat_ref, rstd_ref, i):
        center = value - jnp.mean(value, axis=-1, keepdims=True)
        rstd = lax.rsqrt(jnp.mean(center * center, axis=-1, keepdims=True) + EPS)
        xhat = center * rstd
        xhat_ref[i] = xhat
        rstd_ref[i] = rstd
        return xhat * b.GAIN[index : index + 1, :] + b.SHIFT[index : index + 1, :]

    def add_sum(row, value):
        b.SUM[row : row + 1, :] += column_sum(value)

    def norm_back(index, dy, xhat_ref, rstd_ref, i, bias_row):
        xhat = xhat_ref[i]
        scaled = dy * b.GAIN[index : index + 1, :]
        mean = jnp.mean(scaled, axis=-1, keepdims=True)
        along = jnp.mean(scaled * xhat, axis=-1, keepdims=True)
        dz = (scaled - mean - xhat * along) * rstd_ref[i]
        add_sum(ROW_GAIN + index, dy * xhat)
        add_sum(ROW_SHIFT + index, dy)
        add_sum(bias_row, dz)
        return dz

    def branch_of(total, bias, square):
        branch = total + bias
        add_sum(ROW_SQUARE + square, branch * branch)
        return branch

    def feed(rows, source, index, act_ref, slope_ref):
        for first in range(0, F, 256):
            cols = slice(first, first + 256)
            before = mm(source, b.FFI[:, cols]) + b.FIB[index : index + 1, cols]
            share = 0.5 + 0.5 * lax.erf(before * 0.7071067811865476)
            slope = share + before * jnp.exp(before * before * -0.5) * 0.3989422804014327
            act_ref[rows, cols] = (before * share).astype(BF16)
            slope_ref[rows, cols] = slope.astype(BF16)
        return mm_nt(act_ref[rows, :], b.FFO[...])

    def feed_back(rows, upstream, slope_ref):
        for first in range(0, F, 256):
            cols = slice(first, first + 256)
            dact = mm(upstream, b.FFO[:, cols])
            slope_ref[rows, cols] = (dact * slope_ref[rows, cols].astype(F32)).astype(BF16)
        return mm_nt(slope_ref[rows, :], b.FFI[...])

    block_rows = 128

    def project_enc(i, carry):
        rows = enc_rows(i)
        project(b.X[rows, :], rows, 0, b.Q, b.K, b.V)
        return carry

    lax.fori_loop(0, 4, project_enc, 0)

    def p_store(i):
        slot = i % 2 if isinstance(i, int) else lax.rem(i, jnp.int32(2))
        return pltpu.make_async_copy(b.BIG.at[2 * slot], outs.probs.at[i], sem(at.pst, slot))

    def p_load(i):
        slot = i % 2 if isinstance(i, int) else lax.rem(i, jnp.int32(2))
        return pltpu.make_async_copy(outs.probs.at[i], b.BIG.at[slot], sem(at.pst, slot))

    sum0 = enc_sum(0)

    def att_fwd(i, carry):
        rows = enc_rows(i)
        slot = lax.rem(i, jnp.int32(2))

        @pl.when(i >= 2)
        def _():
            p_store(i - 2).wait()

        def one_block(index, carry):
            shift = pl.multiple_of(index * block_rows, block_rows)
            own = pl.ds(pl.multiple_of(i * CE + shift, block_rows), block_rows)
            q = b.Q[own, :]
            same = b.SEGC[own, :] == b.SEGR[...]
            mixed = jnp.zeros((block_rows, A), F32)
            for h in range(heads):
                scores = mm_nt(only_head(q, h), b.K[...])
                scores = jnp.where(same, scores, NEG)
                expo = jnp.exp(scores - jnp.max(scores, axis=-1, keepdims=True))
                scale = 1.0 / jnp.sum(expo, axis=-1, keepdims=True)
                probs = (expo * scale).astype(BF16)
                b.BIG[2 * slot, pl.ds(pl.multiple_of(h * CE + shift, block_rows), block_rows), :] = probs
                mixed = jnp.where(head_masks[h], mm(probs, b.V[...]), mixed)
            b.O[own, :] = mixed.astype(BF16)
            return carry

        lax.fori_loop(0, CE // block_rows, one_block, 0)
        p_store(i).start()
        pair_send(sum0, i, mm(b.O[rows, :], b.ATO[0]))
        across_send(sum0, i)
        return carry

    lax.fori_loop(0, 4, att_fwd, 0)
    p_store(2).wait()
    p_store(3).wait()

    dsum0 = dec_sum(0)

    def dec_fwd(i, carry):
        rows = dec_chunk(i)
        q = b.QD[rows, :]
        row_index = lax.broadcasted_iota(jnp.int32, (CD, S), 0) + i * CD
        keep = row_index >= lax.broadcasted_iota(jnp.int32, (CD, S), 1)
        mixed = jnp.zeros((CD, A), F32)
        for h in range(heads):
            scores = jnp.where(keep, mm_nt(only_head(q, h), b.KD[...]), NEG)
            expo = jnp.exp(scores - jnp.max(scores, axis=-1, keepdims=True))
            scale = 1.0 / jnp.sum(expo, axis=-1, keepdims=True)
            probs = (expo * scale).astype(BF16)
            b.PD[pl.ds(pl.multiple_of(h * S + i * CD, CD), CD), :] = probs
            mixed = jnp.where(head_masks[h], mm(probs, b.VD[...]), mixed)
        joined = mixed.astype(BF16)
        b.OD[rows, :] = joined
        pair_send(dsum0, i, mm(joined, b.ATO[1]))
        across_send(dsum0, i)
        return carry

    whole = pl.ds(0, S)
    project(b.DX[...], whole, 1, b.QD, b.KD, b.VD)
    lax.fori_loop(0, 2, dec_fwd, 0)

    sum1 = enc_sum(1)
    for copy in load_ffn(0):
        copy.wait()

    def ffn_fwd(i, carry):
        mine = enc_mine(i)
        branch = branch_of(across_take(sum0, i), b.AOB[0:1, :], 0)
        hidden = norm(0, b.X[mine, :].astype(F32) + branch, b.XH0, b.RS0, i)
        b.RES[i] = hidden
        gather_start(at.H1, b.H1, mine, i, hidden.astype(BF16))
        gather_copy(at.H1, b.H1, mine, i).wait()
        rows = enc_rows(i)
        pair_send(sum1, i, feed(rows, b.H1[rows, :], 0, b.ACT0, b.GP0))
        across_send(sum1, i)
        return carry

    lax.fori_loop(0, 4, ffn_fwd, 0)
    for copy in load_ffn(1):
        copy.start()

    def dec_norm(i, carry):
        mine = dec_mine(i)
        branch = branch_of(across_take(dsum0, i), b.AOB[1:2, :], 2)
        hidden = norm(2, b.DX[mine, :].astype(F32) + branch, b.XH2, b.RS2, i)
        b.RESD[i] = hidden
        gather_start(at.G1, b.G1, mine, i, hidden.astype(BF16))
        return carry

    lax.fori_loop(0, 2, dec_norm, 0)
    for i in range(2):
        gather_copy(at.G1, b.G1, dec_mine(i), i).wait()
    project(b.G1[...], whole, 2, b.Q2, None, None)

    def memory_fwd(i, carry):
        mine = enc_mine(i)
        branch = branch_of(across_take(sum1, i), b.FOB[0:1, :], 1)
        hidden = norm(1, b.RES[i] + branch, b.XH1, b.RS1, i)
        add_sum(ROW_SQUARE + 5, hidden * hidden)
        gather_start(at.MEM, b.MEM, mine, i, hidden.astype(BF16))
        gather_copy(at.MEM, b.MEM, mine, i).wait()
        rows = enc_rows(i)
        project(b.MEM[rows, :], rows, 2, None, b.K2, b.V2)
        return carry

    lax.fori_loop(0, 4, memory_fwd, 0)

    dsum1 = dec_sum(1)

    def cross_fwd(i, carry):
        rows = dec_chunk(i)
        q = b.Q2[rows, :]
        mixed = jnp.zeros((CD, A), F32)
        for h in range(heads):
            own = pl.ds(pl.multiple_of(h * S + i * CD, CD), CD)
            weight = b.CNT[own, :].astype(F32)
            scores = jnp.where(weight > 0, mm_nt(only_head(q, h), b.K2[...]), NEG)
            expo = weight * jnp.exp(scores - jnp.max(scores, axis=-1, keepdims=True))
            scale = 1.0 / jnp.sum(expo, axis=-1, keepdims=True)
            probs = (expo * scale).astype(BF16)
            b.CNT[own, :] = probs
            mixed = jnp.where(head_masks[h], mm(probs, b.V2[...]), mixed)
        joined = mixed.astype(BF16)
        b.O2[rows, :] = joined
        pair_send(dsum1, i, mm(joined, b.ATO[2]))
        across_send(dsum1, i)
        return carry

    lax.fori_loop(0, 2, cross_fwd, 0)
    for copy in load_ffn(1):
        copy.wait()

    dsum2 = dec_sum(2)

    def dec_feed(i, carry):
        mine = dec_mine(i)
        branch = branch_of(across_take(dsum1, i), b.AOB[2:3, :], 3)
        hidden = norm(3, b.RESD[i] + branch, b.XH3, b.RS3, i)
        b.RESD[i] = hidden
        gather_start(at.G2, b.G2, mine, i, hidden.astype(BF16))
        gather_copy(at.G2, b.G2, mine, i).wait()
        rows = dec_chunk(i)
        pair_send(dsum2, i, feed(rows, b.G2[rows, :], 1, b.ACT1, b.GP1))
        across_send(dsum2, i)
        return carry

    lax.fori_loop(0, 2, dec_feed, 0)

    dsum3 = dec_sum(3)
    ag_x[3].wait_recv()
    own_copies[3].wait()

    def dec_turn(i, carry):
        mine = dec_mine(i)
        branch = branch_of(across_take(dsum2, i), b.FOB[1:2, :], 4)
        hidden = norm(4, b.RESD[i] + branch, b.XH4, b.RS4, i)
        add_sum(ROW_SQUARE + 6, hidden * hidden)
        b.G3S[i] = hidden.astype(BF16)
        dy = b.DOU[i].astype(F32)
        dz = norm_back(4, dy, b.XH4, b.RS4, i, ROW_FFN_OUT_BIAS + 1)
        b.RESD[i] = dz
        gather_start(at.E5, b.E5, mine, i, dz.astype(BF16))
        gather_copy(at.E5, b.E5, mine, i).wait()
        rows = dec_chunk(i)
        pair_send(dsum3, i, feed_back(rows, b.E5[rows, :], b.GP1))
        across_send(dsum3, i)
        return carry

    lax.fori_loop(0, 2, dec_turn, 0)
    outs.dec_output[...] = b.G3S[x]
    for copy in load_ffn(0):
        copy.start()

    def grad_place(k, j):
        if not p.inside:
            return j
        first, second, third = GRADS[k][2]
        return (j // first % 2) * 4 + (j // second % 2) * 2 + (j // third % 2)

    def transpose_into(source, rows):
        step = min(rows, 256)
        for first in range(0, rows, step):
            b.T[:, first : first + step] = source[first : first + step, :].T

    def grad_columns(k, rows, right, first, count):
        slot = k % SLOTS
        quarter = D // 2
        for a in range(2):
            value = mm(b.T[a * quarter : (a + 1) * quarter, :rows], right[...]).astype(BF16)
            for jj in range(4):
                where = grad_place(k, 4 * a + jj)
                b.GR[slot, where, :, first : first + count] = value[
                    jj * p.block : (jj + 1) * p.block, :
                ]

    def grad_copy(k, step):
        slot = k % SLOTS
        if not p.inside:
            return pltpu.make_async_copy(b.GR.at[slot], outs.grads.at[k], sem(at.grad, k))
        bits = GRADS[k][2]
        target = (flipped(dp, bits[step]), t)
        mine = [bit_of(dp, bit) for bit in bits]
        if step == 0:
            src = b.GR.at[slot, pl.ds(4 * (1 - mine[0]), 4)]
            return remote(src, b.R1.at[slot], at.grad, 3 * k, target)
        if step == 1:
            src = b.GR.at[slot, pl.ds(4 * mine[0] + 2 * (1 - mine[1]), 2)]
            return remote(src, b.R2.at[slot], at.grad, 3 * k + 1, target)
        src = b.GR.at[slot, pl.ds(4 * mine[0] + 2 * mine[1] + 1 - mine[2], 1)]
        return remote(src, b.R3.at[slot], at.grad, 3 * k + 2, target)

    def grad_step(k, step):
        if not p.inside:
            if step == 0:
                grad_copy(k, 0).start()
            if step == 3:
                grad_copy(k, 0).wait()
            return
        slot = k % SLOTS
        mine = [bit_of(dp, bit) for bit in GRADS[k][2]]
        if step > 0:
            grad_copy(k, step - 1).wait()
        if step == 1:
            for j in range(4):
                where = 4 * mine[0] + j
                total = b.GR[slot, where].astype(F32) + b.R1[slot, j].astype(F32)
                b.GR[slot, where] = total.astype(BF16)
        if step == 2:
            for j in range(2):
                where = 4 * mine[0] + 2 * mine[1] + j
                total = b.GR[slot, where].astype(F32) + b.R2[slot, j].astype(F32)
                b.GR[slot, where] = total.astype(BF16)
        if step == 3:
            where = 4 * mine[0] + 2 * mine[1] + mine[2]
            total = b.GR[slot, where].astype(F32) + b.R3[slot, 0].astype(F32)
            kind, index = GRADS[k][:2]
            if kind == ATT:
                for j in range(3):
                    outs.att_in[3 * index + j] = total[:, j * A : (j + 1) * A]
                outs.att_out[index] = total[:, 3 * A : 4 * A]
            elif kind == FFN_IN:
                outs.ffn_in[index] = total
            else:
                outs.ffn_out[index] = total
        if step > 0 and k + SLOTS < len(GRADS):
            later = (flipped(dp, GRADS[k + SLOTS][2][step - 1]), t)
            pl.semaphore_signal(
                free.at[3 * slot + step - 1], inc=1, device_id=later, device_id_type=MESH
            )
        if step < 3:
            if k >= SLOTS:
                pl.semaphore_wait(free.at[3 * slot + step], 1)
            grad_copy(k, step).start()

    def ffn_in_bias(f, dpre_ref):
        def gather_rows(i, total):
            block = dpre_ref[pl.ds(pl.multiple_of(i * CD, CD), CD), :]
            return total + column_sum(block.astype(F32))

        total = lax.fori_loop(0, dpre_ref.shape[0] // CD, gather_rows, jnp.zeros((1, F), F32))
        for owner in range(4):
            row = ROW_FFN_IN_BIAS + 4 * f + owner
            b.SUM[row : row + 1, :] = jnp.where(t == owner, total, 0.0)

    def att_bias(index, dq_ref, dv_ref):
        rows = []
        for ref in (dq_ref, dv_ref):
            rows.append(column_sum(ref[...].astype(F32)))
        for owner in range(4):
            for j in range(2):
                row = BIAS_ROWS * owner + 2 * index + j
                b.BIA[row : row + 1, :A] = jnp.where(t == owner, rows[j], 0.0)

    transpose_into(b.E5, S)
    grad_columns(0, S, b.ACT1, 0, F)
    grad_step(0, 0)
    transpose_into(b.G2, S)
    grad_columns(1, S, b.GP1, 0, F)
    grad_step(1, 0)
    ffn_in_bias(1, b.GP1)

    def dec_back(i, carry):
        mine = dec_mine(i)
        dy = b.RESD[i] + across_take(dsum3, i)
        dz = norm_back(3, dy, b.XH3, b.RS3, i, ROW_ATT_OUT_BIAS + 2)
        b.RESD[i] = dz
        gather_start(at.E4, b.E4, mine, i, dz.astype(BF16))
        return carry

    lax.fori_loop(0, 2, dec_back, 0)
    for i in range(2):
        gather_copy(at.E4, b.E4, dec_mine(i), i).wait()

    def attention_back(up_ref, q_ref, first, k_ref, v_ref, p_ref, d_ref, count, span):
        def one_block(index, carry):
            shift = pl.multiple_of(index * block_rows, block_rows)
            own = pl.ds(pl.multiple_of(first + shift, block_rows), block_rows)
            upstream, q = up_ref[own, :], q_ref[own, :]
            dq = jnp.zeros((block_rows, A), F32)
            for h in range(heads):
                rows = pl.ds(pl.multiple_of(h * count + shift, block_rows), block_rows)
                up = only_head(upstream, h)
                dprobs = mm_nt(up, v_ref[...])
                probs = p_ref[rows, :].astype(F32)
                inner = jnp.sum(probs * dprobs, axis=-1, keepdims=True)
                dscores = (probs * (dprobs - inner)).astype(BF16)
                b.DS[rows, :span] = dscores
                b.QS[rows, :] = only_head(q, h)
                b.DOS[rows, :] = up
                dq = jnp.where(head_masks[h], mm(dscores, k_ref[...]), dq)
            d_ref[own, :] = (dq * 0.125).astype(BF16)
            return carry

        lax.fori_loop(0, count // block_rows, one_block, 0)

    b.UPD[...] = mm_nt(b.E4[...], b.ATO[2]).astype(BF16)
    attention_back(b.UPD, b.Q2, 0, b.K2, b.V2, b.CNT, b.D2, S, R)
    sum2 = enc_sum(2)

    for i in range(4):
        cols = slice(i * CE, (i + 1) * CE)
        b.K2[cols, :] = mm_tn(b.DS[: heads * S, cols], b.QS[: heads * S, :]).astype(BF16)
        b.V2[cols, :] = mm_tn(b.CNT[:, cols], b.DOS[: heads * S, :]).astype(BF16)

    def memory_back(i, carry):
        rows = enc_rows(i)
        part = mm(b.K2[rows, :], b.ATI[7]) + mm(b.V2[rows, :], b.ATI[8])
        pair_send(sum2, i, part)
        across_send(sum2, i)
        return carry

    lax.fori_loop(0, 4, memory_back, 0)
    dsum4 = dec_sum(4)

    def query_back(i, carry):
        rows = dec_chunk(i)
        pair_send(dsum4, i, mm(b.D2[rows, :], b.ATI[6]))
        across_send(dsum4, i)
        return carry

    lax.fori_loop(0, 2, query_back, 0)

    grad_step(0, 1)
    grad_step(1, 1)
    transpose_into(b.G1, S)
    grad_columns(2, S, b.D2, 0, A)
    transpose_into(b.E4, S)
    grad_columns(2, S, b.O2, 3 * A, A)
    transpose_into(b.MEM, R)
    grad_columns(2, R, b.K2, A, A)
    grad_columns(2, R, b.V2, 2 * A, A)
    grad_step(2, 0)
    att_bias(2, b.D2, b.V2)

    sum3 = enc_sum(3)
    for copy in load_ffn(0):
        copy.wait()

    def ffn_back(i, carry):
        mine = enc_mine(i)
        dz = norm_back(1, across_take(sum2, i), b.XH1, b.RS1, i, ROW_FFN_OUT_BIAS)
        b.RES[i] = dz
        gather_start(at.E2, b.E2, mine, i, dz.astype(BF16))
        gather_copy(at.E2, b.E2, mine, i).wait()
        rows = enc_rows(i)
        pair_send(sum3, i, feed_back(rows, b.E2[rows, :], b.GP0))
        across_send(sum3, i)
        return carry

    lax.fori_loop(0, 4, ffn_back, 0)
    grad_step(0, 2)
    grad_step(1, 2)
    grad_step(2, 1)

    def dec_self(i, carry):
        mine = dec_mine(i)
        dy = b.RESD[i] + across_take(dsum4, i)
        dz = norm_back(2, dy, b.XH2, b.RS2, i, ROW_ATT_OUT_BIAS + 1)
        b.RESD[i] = dz
        gather_start(at.E3, b.E3, mine, i, dz.astype(BF16))
        return carry

    lax.fori_loop(0, 2, dec_self, 0)
    for i in range(2):
        gather_copy(at.E3, b.E3, dec_mine(i), i).wait()
    b.UPD[...] = mm_nt(b.E3[...], b.ATO[1]).astype(BF16)
    attention_back(b.UPD, b.QD, 0, b.KD, b.VD, b.PD, b.QD, S, S)
    b.KD[...] = mm_tn(b.DS[: heads * S, :S], b.QS[: heads * S, :]).astype(BF16)
    b.VD[...] = mm_tn(b.PD[...], b.DOS[: heads * S, :]).astype(BF16)

    dsum5 = dec_sum(5)
    for turn in range(2):
        i = 1 - x if turn == 0 else x
        rows = dec_chunk(i)
        part = (
            mm(b.QD[rows, :], b.ATI[3])
            + mm(b.KD[rows, :], b.ATI[4])
            + mm(b.VD[rows, :], b.ATI[5])
        )
        pair_send(dsum5, i, part)
        if turn == 0:
            across_send(dsum5, i)
        else:
            outs.dec_grad[...] = b.RESD[i] + pair_take(dsum5, i)

    grad_step(0, 3)
    transpose_into(b.DX, S)
    grad_columns(3, S, b.QD, 0, A)
    grad_columns(3, S, b.KD, A, A)
    grad_columns(3, S, b.VD, 2 * A, A)
    transpose_into(b.E3, S)
    grad_columns(3, S, b.OD, 3 * A, A)
    grad_step(3, 0)
    att_bias(1, b.QD, b.VD)
    grad_step(1, 3)
    grad_step(2, 2)
    transpose_into(b.E2, R)
    grad_columns(4, R, b.ACT0, 0, F)
    grad_step(4, 0)
    transpose_into(b.H1, R)
    grad_columns(5, R, b.GP0, 0, F)
    grad_step(5, 0)
    ffn_in_bias(0, b.GP0)
    grad_step(2, 3)
    grad_step(3, 1)

    p_load(0).start()
    p_load(1).start()
    b.DK[...] = jnp.zeros((R, A), F32)
    b.DV[...] = jnp.zeros((R, A), F32)

    def att_back(i, carry):
        mine = enc_mine(i)
        slot = lax.rem(i, jnp.int32(2))
        dy = b.RES[i] + across_take(sum3, i)
        dz = norm_back(0, dy, b.XH0, b.RS0, i, ROW_ATT_OUT_BIAS)
        b.RES[i] = dz
        gather_start(at.E1, b.MEM, mine, i, dz.astype(BF16))
        gather_copy(at.E1, b.MEM, mine, i).wait()
        rows = enc_rows(i)
        b.UP[rows, :] = mm_nt(b.MEM[rows, :], b.ATO[0]).astype(BF16)
        p_load(i).wait()
        p_ref = b.BIG.at[slot]
        attention_back(b.UP, b.Q, i * CE, b.K, b.V, p_ref, b.Q, CE, R)
        for j in range(4):
            cols = slice(j * CE, (j + 1) * CE)
            b.DK[cols, :] += mm_tn(b.DS[:, cols], b.QS[...])
            b.DV[cols, :] += mm_tn(b.BIG[slot, :, cols], b.DOS[...])

        @pl.when(i < 2)
        def _():
            p_load(i + 2).start()

        return carry

    lax.fori_loop(0, 4, att_back, 0)
    b.K[...] = b.DK[...].astype(BF16)
    b.V[...] = b.DV[...].astype(BF16)
    att_bias(0, b.Q, b.V)
    transpose_into(b.X, R)
    grad_columns(6, R, b.Q, 0, A)
    grad_columns(6, R, b.K, A, A)
    grad_columns(6, R, b.V, 2 * A, A)
    transpose_into(b.MEM, R)
    grad_columns(6, R, b.O, 3 * A, A)
    grad_step(6, 0)

    steps = [pair, across] + [(flipped(dp, bit), t) for bit in (1, 2, 4)]

    def sum_copy(step):
        return remote(b.SUM, b.SUMR.at[step], at.sum, step, steps[step])

    def bias_copy(step):
        return remote(b.BIA, b.BIAR.at[step], at.sum, 5 + step, steps[step])

    def sum_send(step):
        if p.inside:
            sum_copy(step).start()
            bias_copy(step).start()

    def sum_take(step):
        if p.inside:
            sum_copy(step).wait()
            b.SUM[...] += b.SUMR[step]
            bias_copy(step).wait()
            b.BIA[...] += b.BIAR[step]

    doubled = lax.broadcasted_iota(jnp.int32, (SUM_ROWS, 1), 0) < ROW_FFN_IN_BIAS
    b.SUM[...] = b.SUM[...] * jnp.where(doubled, 0.5, 1.0)
    sum_send(0)

    sum4 = enc_sum(4)
    for turn in range(4):
        i = 2 * (1 - x) + turn if turn < 2 else 2 * x + turn - 2
        rows = enc_rows(i)
        part = (
            mm(b.Q[rows, :], b.ATI[0])
            + mm(b.K[rows, :], b.ATI[1])
            + mm(b.V[rows, :], b.ATI[2])
        )
        pair_send(sum4, i, part)
        if turn < 2:
            across_send(sum4, i)
        else:
            own = (turn - 2) * HE
            outs.enc_grad[own : own + HE, :] = b.RES[i] + pair_take(sum4, i)
    sum_take(0)
    sum_send(1)
    grad_step(3, 2)
    grad_step(4, 1)
    grad_step(5, 1)
    grad_step(6, 1)
    sum_take(1)
    sum_send(2)
    grad_step(3, 3)
    grad_step(4, 2)
    grad_step(5, 2)
    grad_step(6, 2)
    sum_take(2)
    sum_send(3)

    _, dec_across, _, _, _, _, dec_got, _ = dsum5
    dec_across(1 - x).wait_send()
    dec_across(x).wait_recv()
    outs.dec_grad[...] += dec_got[x].astype(F32)
    _, enc_across, _, _, _, _, enc_got, _ = sum4
    for half in range(2):
        enc_across(2 * (1 - x) + half).wait_send()
        enc_across(2 * x + half).wait_recv()
        own = half * HE
        outs.enc_grad[own : own + HE, :] += enc_got[2 * x + half].astype(F32)
    sum_take(3)
    sum_send(4)
    grad_step(4, 3)
    grad_step(5, 3)
    grad_step(6, 3)
    sum_take(4)
    outs.sums[...] = b.SUM[...]
    outs.biases[...] = b.BIA[...]
    for copy in ag_x + ag_p + ag_f:
        copy.wait_send()


BIG_RESULTS = 7


def finish(p, counts, *refs):
    D, A, F = p.D, p.A, p.F
    n = BIG_RESULTS
    sources, (sums, biases) = refs[:n], refs[n : n + 2]
    targets, small, sems = refs[n + 2 : 2 * n + 2], refs[2 * n + 2 : -1], refs[-1]
    copies = [pltpu.make_async_copy(sources[k], targets[k], sems.at[k]) for k in range(n)]
    for copy in copies:
        copy.start()
    att_in_bias, att_out_bias, ffn_in_bias, ffn_out_bias, gain, shift, rms = small
    for owner in range(4):
        first = BIAS_ROWS * owner
        att_in_bias[:, owner * A : (owner + 1) * A] = biases[first : first + 6, :A]
        for f in range(2):
            row = ROW_FFN_IN_BIAS + 4 * f + owner
            ffn_in_bias[f : f + 1, owner * F : (owner + 1) * F] = sums[row : row + 1, :]
    att_out_bias[...] = sums[ROW_ATT_OUT_BIAS : ROW_ATT_OUT_BIAS + 3, :]
    ffn_out_bias[...] = sums[ROW_FFN_OUT_BIAS : ROW_FFN_OUT_BIAS + 2, :]
    gain[...] = sums[ROW_GAIN : ROW_GAIN + 5, :]
    shift[...] = sums[ROW_SHIFT : ROW_SHIFT + 5, :]
    values = jnp.zeros((1, 128), F32)
    lane = lax.broadcasted_iota(jnp.int32, (1, 128), 1)
    for k, count in enumerate(counts):
        row = sums[ROW_SQUARE + k : ROW_SQUARE + k + 1, :]
        values = jnp.where(lane == k, jnp.sum(row, axis=1, keepdims=True) * (1.0 / count), values)
    rms[...] = jnp.sqrt(values)[0, : len(counts)]
    for copy in copies:
        copy.wait()


def body(n_dp, *args):
    named = Inputs(*args)
    named = named._replace(
        att_in=jnp.transpose(named.att_in, (0, 2, 1)),
        att_out=jnp.transpose(named.att_out, (0, 2, 1)),
        retrieval=jnp.transpose(named.retrieval, (0, 2, 1, 3)),
    )
    p = Plan(named, n_dp)
    D, A, F = p.D, p.A, p.F
    shapes = Outputs(
        dec_output=((p.HD, D), BF16),
        enc_grad=((p.CE, D), F32),
        dec_grad=((p.HD, D), F32),
        sums=((SUM_ROWS, D), F32),
        biases=((4 * BIAS_ROWS, 256), F32),
        probs=((4, p.heads * p.CE, p.R), BF16),
    )
    if p.inside:
        shapes = shapes._replace(
            att_in=((9, p.block, A), F32),
            att_out=((3, p.block, A), F32),
            ffn_in=((2, p.block, F), F32),
            ffn_out=((2, p.block, F), F32),
        )
    else:
        shapes = shapes._replace(grads=((7, 8, p.block, D), BF16))
    hbm = pl.BlockSpec(memory_space=pl.ANY)
    vmem = pl.BlockSpec(memory_space=pltpu.VMEM)
    places, made_shapes, out_specs = [], [], []
    for position, value in enumerate(shapes):
        if value is None:
            places.append(None)
            continue
        places.append(len(made_shapes))
        made_shapes.append(jax.ShapeDtypeStruct(*value))
        out_specs.append(hbm if Outputs._fields[position] in (PROBS, ALL_GRADS) else vmem)
    results = pl.pallas_call(
        functools.partial(kernel, p, places),
        out_shape=made_shapes,
        in_specs=[hbm if fetched else vmem for fetched in IN_HBM],
        out_specs=out_specs,
        scratch_shapes=[
            *p.scratch.values(),
            pltpu.SemaphoreType.DMA((p.n_sems,)),
            pltpu.SemaphoreType.REGULAR((3 * SLOTS,)),
        ],
        compiler_params=pltpu.CompilerParams(
            collective_id=0, has_side_effects=True, vmem_limit_bytes=63 * 2**20
        ),
    )(*named)
    made = Outputs(*[None if place is None else results[place] for place in places])
    sums, biases = made.sums, made.biases
    if not p.inside:
        sums, biases = lax.psum((sums, biases), (DP, TENSOR))
        whole = made.grads.reshape(7, D, D).astype(F32)
        parts = lax.psum_scatter(whole, DP, scatter_dimension=1, tiled=True)
        found = {grad[:2]: parts[k] for k, grad in enumerate(GRADS)}
        att = [found[ATT, a] for a in range(3)]
        made = made._replace(
            att_in=jnp.stack([att[a][:, j * A : (j + 1) * A] for a in range(3) for j in range(3)]),
            att_out=jnp.stack([att[a][:, 3 * A : 4 * A] for a in range(3)]),
            ffn_in=jnp.stack([found[FFN_IN, f] for f in range(2)]),
            ffn_out=jnp.stack([found[FFN_OUT, f] for f in range(2)]),
        )
    devices = lax.axis_size(DP) * lax.axis_size(TENSOR)
    enc_count = 1.0 * p.CE * devices * D
    dec_count = 1.0 * p.HD * devices * D
    counts = (enc_count, enc_count, dec_count, dec_count, dec_count, enc_count, dec_count)
    large = (
        made.dec_output,
        made.enc_grad,
        made.dec_grad,
        made.att_in,
        made.att_out,
        made.ffn_in,
        made.ffn_out,
    )
    small = ((6, D), (3, D), (2, 4 * F), (2, D), (5, D), (5, D), (7,))
    done = pl.pallas_call(
        functools.partial(finish, p, counts),
        out_shape=[jax.ShapeDtypeStruct(value.shape, value.dtype) for value in large]
        + [jax.ShapeDtypeStruct(shape, F32) for shape in small],
        in_specs=[vmem] * (BIG_RESULTS + 2),
        out_specs=[hbm] * BIG_RESULTS + [vmem] * len(small),
        scratch_shapes=[pltpu.SemaphoreType.DMA((BIG_RESULTS,))],
    )(*large, sums, biases)
    dec_output, enc_grad, dec_grad, att_in, att_out, ffn_in, ffn_out = done[:BIG_RESULTS]
    att_in_bias, att_out_bias, ffn_in_bias, ffn_out_bias, gain, shift, rms = done[BIG_RESULTS:]
    return (
        dec_output,
        enc_grad,
        dec_grad,
        att_in,
        att_in_bias,
        att_out,
        att_out_bias,
        ffn_in,
        ffn_in_bias,
        ffn_out,
        ffn_out_bias,
        gain,
        shift,
        rms,
    )


def solution(mesh):
    rows = P((DP, TENSOR), None)
    placed = (
        rows,
        rows,
        P(DP, None),
        P(DP, None, TENSOR, None),
        P(None, None, TENSOR),
        P(None, TENSOR),
        P(None, None, TENSOR),
        P(),
        P(None, None, TENSOR),
        P(None, TENSOR),
        P(None, None, TENSOR),
        P(),
        P(),
        P(),
        rows,
    )
    split = P(None, DP, TENSOR)
    return jax.shard_map(
        functools.partial(body, mesh.shape[DP]),
        mesh=mesh,
        in_specs=placed,
        out_specs=(rows, rows, rows, split, P(), split, P(), split, P(), split, P(), P(), P(), P()),
        check_vma=False,
    )
```

time: 1220 us -> 251 us (0.21)
  waiting for transfers between devices: 744 us -> 0 us
  Pallas kernels: 0 us -> 250 us
  other arithmetic: 148 us -> 0 us
  matrix products: 132 us -> 0 us
  local copies, waits for them, and re-layouts: 114 us -> 0 us
  blocking collectives: 37.6 us -> 0 us
  between operations: 16.7 us -> 0.84 us
  loops' own time: 14.2 us -> 0 us
    reduce_scatter x13 -> x0, waiting for transfers between devices: 441 us -> none  [the longest x2 196 us: body(): summed = lax.psum_scatter(whole, 'dp', scatter_dimension=1, tiled=True)]
    pallas_call x0 -> x2, Pallas kernels: none -> 250 us  [the longest x1 246 us: body(): pl.pallas_call(functools.partial(kernel, p, places), out_shape=made_shape...]
    unnamed x23 -> x0, waiting for transfers between devices: 178 us -> none
    dot_general x74 -> x0, matrix products: 132 us -> none  [the longest x16 46 us: product(): return jnp.dot(left, right, preferred_element_type=jnp.float32)]
    reduce_sum x49 -> x0, other arithmetic: 120 us -> none  [the longest x16 85.3 us: one_block(): return jnp.sum(hits, axis=3)]
    psum x1 -> x0, waiting for transfers between devices: 63.4 us -> none  [body(): lax.psum((wide_att, out_bias, wide_ffn, ffn_out_bias_part, gains, shifts,...]
    all_gather x5 -> x0, waiting for transfers between devices: 60.9 us -> none  [the longest x3 41.6 us: rows_gather(): return lax.all_gather(block, 'tensor', axis=0, tiled=True)]
    unnamed x350 -> x0, local copies, waits for them, and re-layouts: 56 us -> none
  transfers between devices with their start and end apart: 21 -> 0, of which waited for: 18 -> 0; matrix products, arithmetic and copies ran while one was open for 23% -> 0% of each run, Pallas kernels for 0% -> 0%
where the time goes in v1:
time: 251 us
  Pallas kernels  250 us (100%)
    pallas_call x1, Pallas kernels, body(): pl.pallas_call(functools.partial(kernel, p, places), out_shape=made_shape...  246 us

profile of v1, /device:TPU:0, one launch (start us, length us, event | category | flops | bytes accessed | tf_op | source)
XLA Modules:
  0.0 251.1 jit_solution(10216282048620088527)
XLA Ops:
  0.7 245.9 %shard_map.254 = (bf16[64,768]{1,0:T(8,128)(2,1)}, f32[256,768]{1,0:T(8,128)}, f32[64,768]{1,0:T(8,128)}, f32[32,768]{1,0:T(8,128)}, f32[32,256]{1,0:T(8,128)}, ...) custom-call(bf16[256,768]{1,0:T(8,128)(2,1)} %refs_0_.1, ...), custom_call_target="tpu_custom_call" | custom-call | tf_op jit(solution)/shard_map/pallas_call | solution.py:1119
  246.5 4.4 %shard_map.255 = (bf16[64,768]{1,0:T(8,128)(2,1)}, f32[256,768]{1,0:T(8,128)}, f32[64,768]{1,0:T(8,128)}, f32[9,96,192]{2,1,0:T(8,128)}, f32[3,96,192]{2,1,0:T(8...) custom-call(bf16[64,768]{1,0:T(8,128)(2,1)} %get-tuple-element.37.re, ...), custom_call_target="tpu_custom_call" | custom-call | tf_op jit(solution)/shard_map/pallas_call | solution.py:1161

commit v2 on v1

--- a/solution.py
+++ b/solution.py
@@ -24,20 +24,39 @@
 ROW_SHIFT = 10
 ROW_SQUARE = 15
 ROW_FFN_IN_BIAS = 24
-SUM_ROWS = 32
-BIAS_ROWS = 8
+ROW_ATT_IN_BIAS = 30
+SUM_ROWS = 40
+LATE_ROWS = 8
+LATE_NORM_ROWS = 3
 
 ATT, FFN_IN, FFN_OUT = range(3)
 GRADS = (
-    (FFN_OUT, 1, (1, 2, 4)),
-    (FFN_IN, 1, (2, 1, 4)),
-    (ATT, 2, (1, 2, 4)),
-    (ATT, 1, (2, 1, 4)),
-    (FFN_OUT, 0, (1, 2, 4)),
-    (FFN_IN, 0, (2, 1, 4)),
-    (ATT, 0, (2, 1, 4)),
+    (FFN_OUT, 1, (2, 1, 4), 0, 0, 2),
+    (FFN_OUT, 1, (1, 4, 2), 0, 2, 4),
+    (FFN_IN, 1, (1, 2, 4), 1, 0, 2),
+    (FFN_IN, 1, (2, 1, 4), 1, 2, 4),
+    (ATT, 2, (2, 1, 4), 2, 0, 2),
+    (ATT, 2, (1, 2, 4), 2, 2, 4),
+    (ATT, 1, (2, 1, 4), 4, 0, 2),
+    (ATT, 1, (1, 2, 4), 4, 2, 4),
+    (FFN_OUT, 0, (1, 2, 4), 3, 0, 2),
+    (FFN_OUT, 0, (2, 1, 4), 3, 2, 4),
+    (FFN_IN, 0, (2, 1, 4), 0, 0, 2),
+    (FFN_IN, 0, (1, 4, 2), 0, 2, 4),
+    (ATT, 0, (1, 4, 2), 1, 0, 2),
+    (ATT, 0, (2, 1, 4), 1, 2, 4),
 )
-SLOTS = 4
+SLOTS = 5
+WHOLE = tuple(grad[:2] for grad in GRADS if grad[4] == 0)
+
+
+def next_in_slot(k):
+    later = range(k + 1, len(GRADS))
+    return [j for j in later if GRADS[j][3:] == GRADS[k][3:]]
+
+
+def waits_for_slot(k):
+    return any(k in next_in_slot(j) for j in range(k))
 
 
 def mm(left, right):
@@ -139,13 +158,16 @@
             RET=((heads, S, self.picks), jnp.int32),
         )
         self.vmem(X=wide, H1=wide, MEM=wide, E2=wide)
-        self.vmem(DX=short, G1=short, G2=short, E5=short, E4=short, E3=short)
+        self.vmem(DX=short, G1=short, G2=short, E5=short, E4=short)
         self.vmem(DOU=dec_half, G3S=dec_half)
-        self.vmem(Q=enc_heads, K=enc_heads, V=enc_heads, O=enc_heads, UP=enc_heads)
+        self.vmem(Q=enc_heads, K=enc_heads, V=enc_heads, O=enc_heads)
         self.vmem(K2=enc_heads, V2=enc_heads)
+        turned = ((A, R), BF16)
+        self.vmem(KT=turned, VT=turned, VT2=turned)
+        self.vmem(KTD=((A, S), BF16), VTD=((A, S), BF16))
         self.vmem(QD=dec_heads, KD=dec_heads, VD=dec_heads, OD=dec_heads, UPD=dec_heads)
         self.vmem(Q2=dec_heads, O2=dec_heads, D2=dec_heads)
-        self.vmem(DK=((R, A), F32), DV=((R, A), F32))
+        self.vmem(DK=((A, R), F32), DV=((A, R), F32))
         self.vmem(BIG=((3, heads * CE, R), BF16), PD=((heads * S, S), BF16), QS=stacked, DOS=stacked)
         self.vmem(ACT0=((R, F), BF16), GP0=((R, F), BF16), ACT1=((S, F), BF16), GP1=((S, F), BF16))
         self.vmem(XH0=enc_float, XH1=enc_float, RES=enc_float)
@@ -162,14 +184,14 @@
                 R2=((SLOTS, 2, self.block, D), BF16),
                 R3=((SLOTS, 1, self.block, D), BF16),
                 SUMR=((5, SUM_ROWS, D), F32),
-                BIAR=((5, 4 * BIAS_ROWS, 256), F32),
+                LATR=((5, LATE_ROWS, D), F32),
             )
-        self.vmem(SUM=((SUM_ROWS, D), F32), BIA=((4 * BIAS_ROWS, 256), F32))
+        self.vmem(SUM=((SUM_ROWS, D), F32), LATE=((LATE_ROWS, D), F32))
         self.vmem(GAIN=((5, D), F32), SHIFT=((5, D), F32))
         self.vmem(AIB=((6, A), F32), AOB=((3, D), F32), FIB=((2, F), F32), FOB=((2, D), F32))
         self.sem(load=8, own=4, ag=24, pst=2, enc=24, dec=12)
         self.sem(H1=8, MEM=8, E2=8, E1=8, G1=4, G2=4, E5=4, E4=4, E3=4)
-        self.sem(grad=42, sum=20)
+        self.sem(grad=84, sum=30)
 
     def vmem(self, **buffers):
         for name, (shape, dtype) in buffers.items():
@@ -186,7 +208,7 @@
     enc_grad: Any
     dec_grad: Any
     sums: Any
-    biases: Any
+    late: Any
     probs: Any
     grads: Any = None
     att_in: Any = None
@@ -203,8 +225,10 @@
     b = SimpleNamespace(**dict(zip(p.scratch, refs[n_in + n_out : -2])))
     sems, free = refs[-2:]
     b.CNT, b.DS = b.BIG.at[1], b.BIG.at[2]
+    b.KT2, b.UP, b.E3 = b.KT, b.K2, b.E5
     D, A, F, R, S, CE, HE, CD, HD = p.D, p.A, p.F, p.R, p.S, p.CE, p.HE, p.CD, p.HD
     heads, at = p.heads, p.at
+    block_rows = 128
 
     t = lax.axis_index(TENSOR)
     dp = lax.axis_index(DP)
@@ -297,7 +321,7 @@
     b.FIB[...] = ins.ffn_in_bias[...].astype(F32)
     b.FOB[...] = ins.ffn_out_bias[...].astype(F32)
     b.SUM[...] = jnp.zeros((SUM_ROWS, D), F32)
-    b.BIA[...] = jnp.zeros((4 * BIAS_ROWS, 256), F32)
+    b.LATE[...] = jnp.zeros((LATE_ROWS, D), F32)
     segments = ins.segment_ids[...].astype(F32)
     order = (0, 2, 1, 3, 4, 6, 5, 7)
     pieces = [segments[:, HE * o : HE * (o + 1)] for o in order]
@@ -318,6 +342,9 @@
 
     def count_block(index, carry):
         base = pl.multiple_of(index * 16, 16)
+        block = lax.div(index, jnp.int32(block_rows // 16))
+        within = lax.rem(index, jnp.int32(block_rows // 16)) * 16
+        first = pl.multiple_of(block * (heads * block_rows) + within, 16)
         for h in range(heads):
             halves = []
             for part in range(2):
@@ -339,36 +366,22 @@
                 halves.append(mm_nt(left, right))
             for k in range(8):
                 value = jnp.concatenate([half[8 * k : 8 * k + 8] for half in halves], axis=0)
-                b.CNT[pl.ds(h * S + base, 16), 128 * k : 128 * (k + 1)] = value.astype(BF16)
+                b.CNT[pl.ds(first + h * block_rows, 16), 128 * k : 128 * (k + 1)] = value.astype(BF16)
         return carry
 
-    half_count = S // 32
-    lax.fori_loop(0, half_count, count_block, 0)
-    ag_x[0].wait_recv()
-    ag_f[0].start()
-    lax.fori_loop(half_count, 2 * half_count, count_block, 0)
-    ag_x[1].wait_recv()
-    ag_f[1].start()
-    ag_x[2].wait_recv()
-    ag_f[2].start()
-    for copy in own_copies[:3]:
-        copy.wait()
-    for copy in ag_p:
-        copy.wait_recv()
-    loads[1].wait()
-    loads[2].wait()
-    for copy in ag_f:
-        copy.wait_recv()
-
-    def project(source, rows, index, target_q, target_k, target_v):
+    def project(source, rows, index, target_q, target_k, target_v, turned_k, turned_v):
         if target_q is not None:
             bias = b.AIB[2 * index : 2 * index + 1, :]
             value = (mm_nt(source, b.ATI[3 * index]) + bias).astype(BF16)
             target_q[rows, :] = value * jnp.asarray(0.125, BF16)
         if target_k is not None:
-            target_k[rows, :] = mm_nt(source, b.ATI[3 * index + 1]).astype(BF16)
+            value = mm_nt(source, b.ATI[3 * index + 1]).astype(BF16)
+            target_k[rows, :] = value
+            turned_k[:, rows] = value.T
             bias = b.AIB[2 * index + 1 : 2 * index + 2, :]
-            target_v[rows, :] = (mm_nt(source, b.ATI[3 * index + 2]) + bias).astype(BF16)
+            value = (mm_nt(source, b.ATI[3 * index + 2]) + bias).astype(BF16)
+            target_v[rows, :] = value
+            turned_v[:, rows] = value.T
 
     def enc_rows(i):
         return pl.ds(pl.multiple_of(i * CE, CE), CE)
@@ -426,10 +439,16 @@
         copy.wait()
         return own[...] + got[i].astype(F32)
 
+    def across_prepare(group, i):
+        sent = group[4]
+        sent[i] = pair_take(group, i).astype(BF16)
+
+    def across_start(group, i):
+        group[1](i).start()
+
     def across_send(group, i):
-        _, across_copy, _, _, sent, _, _, _ = group
-        sent[i] = pair_take(group, i).astype(BF16)
-        across_copy(i).start()
+        across_prepare(group, i)
+        across_start(group, i)
 
     def across_take(group, i):
         _, across_copy, _, _, sent, _, got, _ = group
@@ -460,6 +479,10 @@
         mean = jnp.mean(scaled, axis=-1, keepdims=True)
         along = jnp.mean(scaled * xhat, axis=-1, keepdims=True)
         dz = (scaled - mean - xhat * along) * rstd_ref[i]
+        if index == 0:
+            for row, value in enumerate((dz, dy * xhat, dy)):
+                b.LATE[row : row + 1, :] += column_sum(value)
+            return dz
         add_sum(ROW_GAIN + index, dy * xhat)
         add_sum(ROW_SHIFT + index, dy)
         add_sum(bias_row, dz)
@@ -487,14 +510,28 @@
             slope_ref[rows, cols] = (dact * slope_ref[rows, cols].astype(F32)).astype(BF16)
         return mm_nt(slope_ref[rows, :], b.FFI[...])
 
-    block_rows = 128
-
-    def project_enc(i, carry):
+    def project_enc(i):
         rows = enc_rows(i)
-        project(b.X[rows, :], rows, 0, b.Q, b.K, b.V)
-        return carry
-
-    lax.fori_loop(0, 4, project_enc, 0)
+        project(b.X[rows, :], rows, 0, b.Q, b.K, b.V, b.KT, b.VT)
+
+    for copy in own_copies[:3]:
+        copy.wait()
+    loads[1].wait()
+    loads[2].wait()
+    ag_p[0].wait_recv()
+    project_enc(2 * x)
+    ag_p[1].wait_recv()
+    project_enc(2 * x + 1)
+    lax.fori_loop(0, 4, count_block, 0)
+    ag_x[0].wait_recv()
+    ag_f[0].start()
+    lax.fori_loop(4, 8, count_block, 0)
+    ag_x[1].wait_recv()
+    ag_f[1].start()
+    ag_f[0].wait_recv()
+    project_enc(2 - 2 * x)
+    ag_f[1].wait_recv()
+    project_enc(3 - 2 * x)
 
     def p_store(i):
         slot = i % 2 if isinstance(i, int) else lax.rem(i, jnp.int32(2))
@@ -504,66 +541,87 @@
         slot = i % 2 if isinstance(i, int) else lax.rem(i, jnp.int32(2))
         return pltpu.make_async_copy(outs.probs.at[i], b.BIG.at[slot], sem(at.pst, slot))
 
+    stack = heads * block_rows
+
+    def heads_stacked(values):
+        return jnp.concatenate([only_head(values, h) for h in range(heads)], axis=0)
+
+    def heads_joined(values):
+        joined = values[:block_rows]
+        for h in range(1, heads):
+            own = values[h * block_rows : (h + 1) * block_rows]
+            joined = jnp.where(head_masks[h], own, joined)
+        return joined
+
+    def attend(q, kt_ref, v_ref, p_ref, first, same):
+        scores = mm(heads_stacked(q), kt_ref[...])
+        for h in range(heads):
+            rows = pl.ds(pl.multiple_of(first + h * block_rows, block_rows), block_rows)
+            own = scores[h * block_rows : (h + 1) * block_rows]
+            if same is None:
+                weight = p_ref[rows, :].astype(F32)
+                own = jnp.where(weight > 0, own, NEG)
+                expo = weight * jnp.exp(own - jnp.max(own, axis=-1, keepdims=True))
+            else:
+                own = jnp.where(same, own, NEG)
+                expo = jnp.exp(own - jnp.max(own, axis=-1, keepdims=True))
+            scale = 1.0 / jnp.sum(expo, axis=-1, keepdims=True)
+            p_ref[rows, :] = (expo * scale).astype(BF16)
+        probs = p_ref[pl.ds(pl.multiple_of(first, block_rows), stack), :]
+        return heads_joined(mm(probs, v_ref[...])).astype(BF16)
+
     sum0 = enc_sum(0)
 
     def att_fwd(i, carry):
-        rows = enc_rows(i)
         slot = lax.rem(i, jnp.int32(2))
 
         @pl.when(i >= 2)
         def _():
             p_store(i - 2).wait()
 
+        @pl.when(i == 2)
+        def _():
+            ag_x[2].wait_recv()
+            ag_f[2].start()
+
         def one_block(index, carry):
-            shift = pl.multiple_of(index * block_rows, block_rows)
-            own = pl.ds(pl.multiple_of(i * CE + shift, block_rows), block_rows)
-            q = b.Q[own, :]
+            own = pl.ds(pl.multiple_of(i * CE + index * block_rows, block_rows), block_rows)
             same = b.SEGC[own, :] == b.SEGR[...]
-            mixed = jnp.zeros((block_rows, A), F32)
-            for h in range(heads):
-                scores = mm_nt(only_head(q, h), b.K[...])
-                scores = jnp.where(same, scores, NEG)
-                expo = jnp.exp(scores - jnp.max(scores, axis=-1, keepdims=True))
-                scale = 1.0 / jnp.sum(expo, axis=-1, keepdims=True)
-                probs = (expo * scale).astype(BF16)
-                b.BIG[2 * slot, pl.ds(pl.multiple_of(h * CE + shift, block_rows), block_rows), :] = probs
-                mixed = jnp.where(head_masks[h], mm(probs, b.V[...]), mixed)
-            b.O[own, :] = mixed.astype(BF16)
+            p_ref = b.BIG.at[2 * slot]
+            b.O[own, :] = attend(b.Q[own, :], b.KT, b.V, p_ref, index * stack, same)
+
+            @pl.when((index == 0) & (i > 0))
+            def _():
+                across_send(sum0, i - 1)
+
             return carry
 
         lax.fori_loop(0, CE // block_rows, one_block, 0)
         p_store(i).start()
-        pair_send(sum0, i, mm(b.O[rows, :], b.ATO[0]))
-        across_send(sum0, i)
+        pair_send(sum0, i, mm(b.O[enc_rows(i), :], b.ATO[0]))
         return carry
 
     lax.fori_loop(0, 4, att_fwd, 0)
+
+    dsum0 = dec_sum(0)
+    whole = pl.ds(0, S)
+    ag_p[2].wait_recv()
+    ag_f[2].wait_recv()
+    project(b.DX[...], whole, 1, b.QD, b.KD, b.VD, b.KTD, b.VTD)
+    across_send(sum0, 3)
     p_store(2).wait()
     p_store(3).wait()
 
-    dsum0 = dec_sum(0)
-
     def dec_fwd(i, carry):
         rows = dec_chunk(i)
-        q = b.QD[rows, :]
         row_index = lax.broadcasted_iota(jnp.int32, (CD, S), 0) + i * CD
         keep = row_index >= lax.broadcasted_iota(jnp.int32, (CD, S), 1)
-        mixed = jnp.zeros((CD, A), F32)
-        for h in range(heads):
-            scores = jnp.where(keep, mm_nt(only_head(q, h), b.KD[...]), NEG)
-            expo = jnp.exp(scores - jnp.max(scores, axis=-1, keepdims=True))
-            scale = 1.0 / jnp.sum(expo, axis=-1, keepdims=True)
-            probs = (expo * scale).astype(BF16)
-            b.PD[pl.ds(pl.multiple_of(h * S + i * CD, CD), CD), :] = probs
-            mixed = jnp.where(head_masks[h], mm(probs, b.VD[...]), mixed)
-        joined = mixed.astype(BF16)
+        joined = attend(b.QD[rows, :], b.KTD, b.VD, b.PD, i * stack, keep)
         b.OD[rows, :] = joined
         pair_send(dsum0, i, mm(joined, b.ATO[1]))
         across_send(dsum0, i)
         return carry
 
-    whole = pl.ds(0, S)
-    project(b.DX[...], whole, 1, b.QD, b.KD, b.VD)
     lax.fori_loop(0, 2, dec_fwd, 0)
 
     sum1 = enc_sum(1)
@@ -576,9 +634,11 @@
         hidden = norm(0, b.X[mine, :].astype(F32) + branch, b.XH0, b.RS0, i)
         b.RES[i] = hidden
         gather_start(at.H1, b.H1, mine, i, hidden.astype(BF16))
+        count_block(8 + 2 * i, 0)
         gather_copy(at.H1, b.H1, mine, i).wait()
         rows = enc_rows(i)
         pair_send(sum1, i, feed(rows, b.H1[rows, :], 0, b.ACT0, b.GP0))
+        count_block(9 + 2 * i, 0)
         across_send(sum1, i)
         return carry
 
@@ -597,7 +657,7 @@
     lax.fori_loop(0, 2, dec_norm, 0)
     for i in range(2):
         gather_copy(at.G1, b.G1, dec_mine(i), i).wait()
-    project(b.G1[...], whole, 2, b.Q2, None, None)
+    project(b.G1[...], whole, 2, b.Q2, None, None, None, None)
 
     def memory_fwd(i, carry):
         mine = enc_mine(i)
@@ -607,7 +667,7 @@
         gather_start(at.MEM, b.MEM, mine, i, hidden.astype(BF16))
         gather_copy(at.MEM, b.MEM, mine, i).wait()
         rows = enc_rows(i)
-        project(b.MEM[rows, :], rows, 2, None, b.K2, b.V2)
+        project(b.MEM[rows, :], rows, 2, None, b.K2, b.V2, b.KT2, b.VT2)
         return carry
 
     lax.fori_loop(0, 4, memory_fwd, 0)
@@ -616,18 +676,7 @@
 
     def cross_fwd(i, carry):
         rows = dec_chunk(i)
-        q = b.Q2[rows, :]
-        mixed = jnp.zeros((CD, A), F32)
-        for h in range(heads):
-            own = pl.ds(pl.multiple_of(h * S + i * CD, CD), CD)
-            weight = b.CNT[own, :].astype(F32)
-            scores = jnp.where(weight > 0, mm_nt(only_head(q, h), b.K2[...]), NEG)
-            expo = weight * jnp.exp(scores - jnp.max(scores, axis=-1, keepdims=True))
-            scale = 1.0 / jnp.sum(expo, axis=-1, keepdims=True)
-            probs = (expo * scale).astype(BF16)
-            b.CNT[own, :] = probs
-            mixed = jnp.where(head_masks[h], mm(probs, b.V2[...]), mixed)
-        joined = mixed.astype(BF16)
+        joined = attend(b.Q2[rows, :], b.KT2, b.V2, b.CNT, i * stack, None)
         b.O2[rows, :] = joined
         pair_send(dsum1, i, mm(joined, b.ATO[2]))
         across_send(dsum1, i)
@@ -689,74 +738,80 @@
         for first in range(0, rows, step):
             b.T[:, first : first + step] = source[first : first + step, :].T
 
-    def grad_columns(k, rows, right, first, count):
-        slot = k % SLOTS
+    def grad_columns(half, rows, right, first):
+        slot = GRADS[half][3]
         quarter = D // 2
+        count = right.shape[1]
         for a in range(2):
             value = mm(b.T[a * quarter : (a + 1) * quarter, :rows], right[...]).astype(BF16)
-            for jj in range(4):
-                where = grad_place(k, 4 * a + jj)
-                b.GR[slot, where, :, first : first + count] = value[
-                    jj * p.block : (jj + 1) * p.block, :
-                ]
+            for k in (half, half + 1):
+                low, high = max(first, GRADS[k][4] * A), min(first + count, GRADS[k][5] * A)
+                for jj in range(4 if low < high else 0):
+                    where = grad_place(k, 4 * a + jj)
+                    rows_own = slice(jj * p.block, (jj + 1) * p.block)
+                    b.GR[slot, where, :, low:high] = value[rows_own, low - first : high - first]
+
+    def both_steps(half, step):
+        grad_step(half, step)
+        grad_step(half + 1, step)
 
     def grad_copy(k, step):
-        slot = k % SLOTS
+        _, _, bits, slot, low, high = GRADS[k]
+        cols = pl.ds(low * A, (high - low) * A)
         if not p.inside:
-            return pltpu.make_async_copy(b.GR.at[slot], outs.grads.at[k], sem(at.grad, k))
-        bits = GRADS[k][2]
+            whole_index = WHOLE.index(GRADS[k][:2])
+            return pltpu.make_async_copy(b.GR.at[slot], outs.grads.at[whole_index], sem(at.grad, k))
         target = (flipped(dp, bits[step]), t)
         mine = [bit_of(dp, bit) for bit in bits]
         if step == 0:
-            src = b.GR.at[slot, pl.ds(4 * (1 - mine[0]), 4)]
-            return remote(src, b.R1.at[slot], at.grad, 3 * k, target)
-        if step == 1:
-            src = b.GR.at[slot, pl.ds(4 * mine[0] + 2 * (1 - mine[1]), 2)]
-            return remote(src, b.R2.at[slot], at.grad, 3 * k + 1, target)
-        src = b.GR.at[slot, pl.ds(4 * mine[0] + 2 * mine[1] + 1 - mine[2], 1)]
-        return remote(src, b.R3.at[slot], at.grad, 3 * k + 2, target)
+            first, count, got = 4 * (1 - mine[0]), 4, b.R1
+        elif step == 1:
+            first, count, got = 4 * mine[0] + 2 * (1 - mine[1]), 2, b.R2
+        else:
+            first, count, got = 4 * mine[0] + 2 * mine[1] + 1 - mine[2], 1, b.R3
+        src = b.GR.at[slot, pl.ds(first, count), :, cols]
+        return remote(src, got.at[slot, :, :, cols], at.grad, 3 * k + step, target)
 
     def grad_step(k, step):
+        kind, index, bits, slot, low, high = GRADS[k]
         if not p.inside:
-            if step == 0:
+            if high == 4 and step == 0:
                 grad_copy(k, 0).start()
-            if step == 3:
+            if high == 4 and step == 3:
                 grad_copy(k, 0).wait()
             return
-        slot = k % SLOTS
-        mine = [bit_of(dp, bit) for bit in GRADS[k][2]]
+        cols = slice(low * A, high * A)
+        mine = [bit_of(dp, bit) for bit in bits]
         if step > 0:
             grad_copy(k, step - 1).wait()
-        if step == 1:
-            for j in range(4):
-                where = 4 * mine[0] + j
-                total = b.GR[slot, where].astype(F32) + b.R1[slot, j].astype(F32)
-                b.GR[slot, where] = total.astype(BF16)
-        if step == 2:
-            for j in range(2):
-                where = 4 * mine[0] + 2 * mine[1] + j
-                total = b.GR[slot, where].astype(F32) + b.R2[slot, j].astype(F32)
-                b.GR[slot, where] = total.astype(BF16)
+        if step in (1, 2):
+            got = b.R1 if step == 1 else b.R2
+            base = 4 * mine[0] if step == 1 else 4 * mine[0] + 2 * mine[1]
+            for j in range(got.shape[1]):
+                total = b.GR[slot, base + j, :, cols].astype(F32) + got[slot, j, :, cols].astype(F32)
+                b.GR[slot, base + j, :, cols] = total.astype(BF16)
         if step == 3:
-            where = 4 * mine[0] + 2 * mine[1] + mine[2]
-            total = b.GR[slot, where].astype(F32) + b.R3[slot, 0].astype(F32)
-            kind, index = GRADS[k][:2]
+            place_own = 4 * mine[0] + 2 * mine[1] + mine[2]
+            total = b.GR[slot, place_own, :, cols].astype(F32) + b.R3[slot, 0, :, cols].astype(F32)
             if kind == ATT:
-                for j in range(3):
-                    outs.att_in[3 * index + j] = total[:, j * A : (j + 1) * A]
-                outs.att_out[index] = total[:, 3 * A : 4 * A]
+                for j in range(low, high):
+                    part = total[:, (j - low) * A : (j - low + 1) * A]
+                    if j < 3:
+                        outs.att_in[3 * index + j] = part
+                    else:
+                        outs.att_out[index] = part
             elif kind == FFN_IN:
-                outs.ffn_in[index] = total
+                outs.ffn_in[index, :, cols] = total
             else:
-                outs.ffn_out[index] = total
-        if step > 0 and k + SLOTS < len(GRADS):
-            later = (flipped(dp, GRADS[k + SLOTS][2][step - 1]), t)
-            pl.semaphore_signal(
-                free.at[3 * slot + step - 1], inc=1, device_id=later, device_id_type=MESH
-            )
+                outs.ffn_out[index, :, cols] = total
+        if step > 0:
+            for j in next_in_slot(k):
+                later = (flipped(dp, GRADS[j][2][step - 1]), t)
+                free_sem = free.at[3 * j + step - 1]
+                pl.semaphore_signal(free_sem, inc=1, device_id=later, device_id_type=MESH)
         if step < 3:
-            if k >= SLOTS:
-                pl.semaphore_wait(free.at[3 * slot + step], 1)
+            if waits_for_slot(k):
+                pl.semaphore_wait(free.at[3 * k + step], 1)
             grad_copy(k, step).start()
 
     def ffn_in_bias(f, dpre_ref):
@@ -773,17 +828,18 @@
         rows = []
         for ref in (dq_ref, dv_ref):
             rows.append(column_sum(ref[...].astype(F32)))
+        table, first = (b.LATE, LATE_NORM_ROWS) if index == 0 else (b.SUM, ROW_ATT_IN_BIAS + 2 * index)
         for owner in range(4):
             for j in range(2):
-                row = BIAS_ROWS * owner + 2 * index + j
-                b.BIA[row : row + 1, :A] = jnp.where(t == owner, rows[j], 0.0)
+                cols = slice(owner * A, (owner + 1) * A)
+                table[first + j : first + j + 1, cols] = jnp.where(t == owner, rows[j], 0.0)
 
     transpose_into(b.E5, S)
-    grad_columns(0, S, b.ACT1, 0, F)
-    grad_step(0, 0)
+    grad_columns(0, S, b.ACT1, 0)
+    both_steps(0, 0)
     transpose_into(b.G2, S)
-    grad_columns(1, S, b.GP1, 0, F)
-    grad_step(1, 0)
+    grad_columns(2, S, b.GP1, 0)
+    both_steps(2, 0)
     ffn_in_bias(1, b.GP1)
 
     def dec_back(i, carry):
@@ -798,66 +854,72 @@
     for i in range(2):
         gather_copy(at.E4, b.E4, dec_mine(i), i).wait()
 
-    def attention_back(up_ref, q_ref, first, k_ref, v_ref, p_ref, d_ref, count, span):
-        def one_block(index, carry):
-            shift = pl.multiple_of(index * block_rows, block_rows)
-            own = pl.ds(pl.multiple_of(first + shift, block_rows), block_rows)
-            upstream, q = up_ref[own, :], q_ref[own, :]
-            dq = jnp.zeros((block_rows, A), F32)
+    def attention_back(up_ref, q_ref, o_ref, first, k_ref, vt_ref, p_ref, d_ref, count, span):
+        def one_block(index):
+            own = pl.ds(pl.multiple_of(first + index * block_rows, block_rows), block_rows)
+            stacked = slice(index * stack, (index + 1) * stack)
+            upstream = up_ref[own, :]
+            along = upstream.astype(F32) * o_ref[own, :].astype(F32)
+            ups = heads_stacked(upstream)
+            b.DOS[stacked, :] = ups
+            b.QS[stacked, :] = heads_stacked(q_ref[own, :])
+            dprobs = mm(ups, vt_ref[...])
             for h in range(heads):
-                rows = pl.ds(pl.multiple_of(h * count + shift, block_rows), block_rows)
-                up = only_head(upstream, h)
-                dprobs = mm_nt(up, v_ref[...])
-                probs = p_ref[rows, :].astype(F32)
-                inner = jnp.sum(probs * dprobs, axis=-1, keepdims=True)
-                dscores = (probs * (dprobs - inner)).astype(BF16)
-                b.DS[rows, :span] = dscores
-                b.QS[rows, :] = only_head(q, h)
-                b.DOS[rows, :] = up
-                dq = jnp.where(head_masks[h], mm(dscores, k_ref[...]), dq)
+                rows = slice(index * stack + h * block_rows, index * stack + (h + 1) * block_rows)
+                inner = jnp.sum(jnp.where(head_masks[h], along, 0.0), axis=-1, keepdims=True)
+                part = dprobs[h * block_rows : (h + 1) * block_rows] - inner
+                b.DS[rows, :span] = (p_ref[rows, :].astype(F32) * part).astype(BF16)
+            dq = heads_joined(mm(b.DS[stacked, :span], k_ref[...]))
             d_ref[own, :] = (dq * 0.125).astype(BF16)
-            return carry
-
-        lax.fori_loop(0, count // block_rows, one_block, 0)
+
+        for index in range(count // block_rows):
+            one_block(index)
 
     b.UPD[...] = mm_nt(b.E4[...], b.ATO[2]).astype(BF16)
-    attention_back(b.UPD, b.Q2, 0, b.K2, b.V2, b.CNT, b.D2, S, R)
+    attention_back(b.UPD, b.Q2, b.O2, jnp.int32(0), b.K2, b.VT2, b.CNT, b.D2, S, R)
     sum2 = enc_sum(2)
 
     for i in range(4):
         cols = slice(i * CE, (i + 1) * CE)
-        b.K2[cols, :] = mm_tn(b.DS[: heads * S, cols], b.QS[: heads * S, :]).astype(BF16)
-        b.V2[cols, :] = mm_tn(b.CNT[:, cols], b.DOS[: heads * S, :]).astype(BF16)
-
-    def memory_back(i, carry):
-        rows = enc_rows(i)
-        part = mm(b.K2[rows, :], b.ATI[7]) + mm(b.V2[rows, :], b.ATI[8])
-        pair_send(sum2, i, part)
-        across_send(sum2, i)
-        return carry
-
-    lax.fori_loop(0, 4, memory_back, 0)
+        b.K2[cols, :] = mm_tn(b.QS[: heads * S, :], b.DS[: heads * S, cols]).astype(BF16).T
+        b.V2[cols, :] = mm_tn(b.DOS[: heads * S, :], b.CNT[:, cols]).astype(BF16).T
+
+    def memory_back(i):
+        rows = slice(i * CE, (i + 1) * CE)
+        return mm(b.K2[rows, :], b.ATI[7]) + mm(b.V2[rows, :], b.ATI[8])
+
+    def query_back(i):
+        return mm(b.D2[i * CD : (i + 1) * CD, :], b.ATI[6])
+
     dsum4 = dec_sum(4)
-
-    def query_back(i, carry):
-        rows = dec_chunk(i)
-        pair_send(dsum4, i, mm(b.D2[rows, :], b.ATI[6]))
-        across_send(dsum4, i)
-        return carry
-
-    lax.fori_loop(0, 2, query_back, 0)
-
-    grad_step(0, 1)
+    pair_send(sum2, 0, memory_back(0))
+    part = memory_back(1)
+    across_send(sum2, 0)
+    pair_send(sum2, 1, part)
+    transpose_into(b.G1, S)
+    grad_columns(4, S, b.D2, 0)
+    across_send(sum2, 1)
+    transpose_into(b.MEM, R)
+    grad_columns(4, R, b.K2, A)
+    grad_step(4, 0)
+    grad_columns(4, R, b.V2, 2 * A)
+    transpose_into(b.E4, S)
+    grad_columns(4, S, b.O2, 3 * A)
+    grad_step(5, 0)
     grad_step(1, 1)
-    transpose_into(b.G1, S)
-    grad_columns(2, S, b.D2, 0, A)
-    transpose_into(b.E4, S)
-    grad_columns(2, S, b.O2, 3 * A, A)
-    transpose_into(b.MEM, R)
-    grad_columns(2, R, b.K2, A, A)
-    grad_columns(2, R, b.V2, 2 * A, A)
-    grad_step(2, 0)
+    sends = [(dsum4, i, query_back) for i in (0, 1)]
+    sends += [(sum2, i, memory_back) for i in (2, 3)]
+    before = None
+    for group, i, part_of in sends:
+        if group is sum2 and i == 2:
+            grad_step(0, 1)
+        part = part_of(i)
+        if before is not None:
+            across_send(*before)
+        pair_send(group, i, part)
+        before = (group, i)
     att_bias(2, b.D2, b.V2)
+    across_send(*before)
 
     sum3 = enc_sum(3)
     for copy in load_ffn(0):
@@ -865,19 +927,38 @@
 
     def ffn_back(i, carry):
         mine = enc_mine(i)
-        dz = norm_back(1, across_take(sum2, i), b.XH1, b.RS1, i, ROW_FFN_OUT_BIAS)
+
+        @pl.when(i == 1)
+        def _():
+            grad_step(5, 1)
+
+        dy = across_take(sum2, i)
+
+        @pl.when(i == 0)
+        def _():
+            grad_step(2, 1)
+
+        @pl.when(i >= 2)
+        def _():
+            across_start(sum3, i - 2)
+
+        dz = norm_back(1, dy, b.XH1, b.RS1, i, ROW_FFN_OUT_BIAS)
         b.RES[i] = dz
         gather_start(at.E2, b.E2, mine, i, dz.astype(BF16))
+
+        @pl.when(i >= 1)
+        def _():
+            across_prepare(sum3, i - 1)
+
         gather_copy(at.E2, b.E2, mine, i).wait()
         rows = enc_rows(i)
         pair_send(sum3, i, feed_back(rows, b.E2[rows, :], b.GP0))
-        across_send(sum3, i)
         return carry
 
-    lax.fori_loop(0, 4, ffn_back, 0)
+    lax.fori_loop(0, 2, ffn_back, 0)
+    grad_step(1, 2)
+    grad_step(3, 1)
     grad_step(0, 2)
-    grad_step(1, 2)
-    grad_step(2, 1)
 
     def dec_self(i, carry):
         mine = dec_mine(i)
@@ -891,7 +972,7 @@
     for i in range(2):
         gather_copy(at.E3, b.E3, dec_mine(i), i).wait()
     b.UPD[...] = mm_nt(b.E3[...], b.ATO[1]).astype(BF16)
-    attention_back(b.UPD, b.QD, 0, b.KD, b.VD, b.PD, b.QD, S, S)
+    attention_back(b.UPD, b.QD, b.OD, jnp.int32(0), b.KD, b.VTD, b.PD, b.QD, S, S)
     b.KD[...] = mm_tn(b.DS[: heads * S, :S], b.QS[: heads * S, :]).astype(BF16)
     b.VD[...] = mm_tn(b.PD[...], b.DOS[: heads * S, :]).astype(BF16)
 
@@ -910,31 +991,62 @@
         else:
             outs.dec_grad[...] = b.RESD[i] + pair_take(dsum5, i)
 
+    transpose_into(b.DX, S)
+    grad_columns(6, S, b.QD, 0)
+    grad_columns(6, S, b.KD, A)
+    grad_step(4, 1)
+    grad_step(6, 0)
+    grad_columns(6, S, b.VD, 2 * A)
+    transpose_into(b.E3, S)
+    grad_columns(6, S, b.OD, 3 * A)
+    grad_step(2, 2)
+    grad_step(7, 0)
+    att_bias(1, b.QD, b.VD)
+    lax.fori_loop(2, 4, ffn_back, 0)
+    across_start(sum3, 2)
+    across_send(sum3, 3)
+    grad_step(1, 3)
+
+    steps = [pair, across] + [(flipped(dp, bit), t) for bit in (1, 2, 4)]
+
+    def total_copy(buffer, got, first, step):
+        return remote(buffer, got.at[step], at.sum, first + step, steps[step])
+
+    def total_step(buffer, got, first, step):
+        if not p.inside:
+            return
+        if step > 0:
+            total_copy(buffer, got, first, step - 1).wait()
+            buffer[...] += got[step - 1]
+        if step < len(steps):
+            total_copy(buffer, got, first, step).start()
+
+    def early_step(step):
+        total_step(b.SUM, b.SUMR if p.inside else None, 0, step)
+
+    def late_step(step):
+        total_step(b.LATE, b.LATR if p.inside else None, 5, step)
+
+    doubled = lax.broadcasted_iota(jnp.int32, (SUM_ROWS, 1), 0) < ROW_FFN_IN_BIAS
+    ffn_in_bias(0, b.GP0)
+    b.SUM[...] = b.SUM[...] * jnp.where(doubled, 0.5, 1.0)
+    transpose_into(b.E2, R)
+    grad_columns(8, R, b.ACT0, 0)
+    both_steps(8, 0)
+    grad_step(6, 1)
     grad_step(0, 3)
-    transpose_into(b.DX, S)
-    grad_columns(3, S, b.QD, 0, A)
-    grad_columns(3, S, b.KD, A, A)
-    grad_columns(3, S, b.VD, 2 * A, A)
-    transpose_into(b.E3, S)
-    grad_columns(3, S, b.OD, 3 * A, A)
-    grad_step(3, 0)
-    att_bias(1, b.QD, b.VD)
-    grad_step(1, 3)
-    grad_step(2, 2)
-    transpose_into(b.E2, R)
-    grad_columns(4, R, b.ACT0, 0, F)
-    grad_step(4, 0)
     transpose_into(b.H1, R)
-    grad_columns(5, R, b.GP0, 0, F)
-    grad_step(5, 0)
-    ffn_in_bias(0, b.GP0)
+    grad_columns(10, R, b.GP0, 0)
+    grad_step(3, 2)
+    early_step(0)
+    both_steps(10, 0)
     grad_step(2, 3)
-    grad_step(3, 1)
+    grad_step(4, 2)
 
     p_load(0).start()
     p_load(1).start()
-    b.DK[...] = jnp.zeros((R, A), F32)
-    b.DV[...] = jnp.zeros((R, A), F32)
+    b.DK[...] = jnp.zeros((A, R), F32)
+    b.DV[...] = jnp.zeros((A, R), F32)
 
     def att_back(i, carry):
         mine = enc_mine(i)
@@ -943,16 +1055,32 @@
         dz = norm_back(0, dy, b.XH0, b.RS0, i, ROW_ATT_OUT_BIAS)
         b.RES[i] = dz
         gather_start(at.E1, b.MEM, mine, i, dz.astype(BF16))
+
+        @pl.when(i == 0)
+        def _():
+            grad_step(7, 1)
+            early_step(1)
+            grad_step(5, 2)
+
+        @pl.when(i == 2)
+        def _():
+            grad_step(6, 2)
+
+        @pl.when(i == 3)
+        def _():
+            grad_step(11, 1)
+            grad_step(9, 1)
+
         gather_copy(at.E1, b.MEM, mine, i).wait()
         rows = enc_rows(i)
         b.UP[rows, :] = mm_nt(b.MEM[rows, :], b.ATO[0]).astype(BF16)
         p_load(i).wait()
         p_ref = b.BIG.at[slot]
-        attention_back(b.UP, b.Q, i * CE, b.K, b.V, p_ref, b.Q, CE, R)
-        for j in range(4):
-            cols = slice(j * CE, (j + 1) * CE)
-            b.DK[cols, :] += mm_tn(b.DS[:, cols], b.QS[...])
-            b.DV[cols, :] += mm_tn(b.BIG[slot, :, cols], b.DOS[...])
+        attention_back(b.UP, b.Q, b.O, i * CE, b.K, b.VT, p_ref, b.Q, CE, R)
+        for j in range(2):
+            cols = slice(2 * j * CE, 2 * (j + 1) * CE)
+            b.DK[:, cols] += mm_tn(b.QS[...], b.DS[:, cols])
+            b.DV[:, cols] += mm_tn(b.DOS[...], b.BIG[slot, :, cols])
 
         @pl.when(i < 2)
         def _():
@@ -961,40 +1089,30 @@
         return carry
 
     lax.fori_loop(0, 4, att_back, 0)
-    b.K[...] = b.DK[...].astype(BF16)
-    b.V[...] = b.DV[...].astype(BF16)
+    for j in range(4):
+        cols = slice(j * CE, (j + 1) * CE)
+        b.K[cols, :] = b.DK[:, cols].astype(BF16).T
+        b.V[cols, :] = b.DV[:, cols].astype(BF16).T
+    grad_step(8, 1)
+    grad_step(3, 3)
     att_bias(0, b.Q, b.V)
+    norm_rows = lax.broadcasted_iota(jnp.int32, (LATE_ROWS, 1), 0) < LATE_NORM_ROWS
+    b.LATE[...] = b.LATE[...] * jnp.where(norm_rows, 0.5, 1.0)
+    late_step(0)
+    grad_step(5, 3)
+    grad_step(6, 3)
+    early_step(2)
     transpose_into(b.X, R)
-    grad_columns(6, R, b.Q, 0, A)
-    grad_columns(6, R, b.K, A, A)
-    grad_columns(6, R, b.V, 2 * A, A)
+    grad_columns(12, R, b.Q, 0)
+    grad_columns(12, R, b.K, A)
+    grad_step(12, 0)
+    late_step(1)
+    grad_columns(12, R, b.V, 2 * A)
     transpose_into(b.MEM, R)
-    grad_columns(6, R, b.O, 3 * A, A)
-    grad_step(6, 0)
-
-    steps = [pair, across] + [(flipped(dp, bit), t) for bit in (1, 2, 4)]
-
-    def sum_copy(step):
-        return remote(b.SUM, b.SUMR.at[step], at.sum, step, steps[step])
-
-    def bias_copy(step):
-        return remote(b.BIA, b.BIAR.at[step], at.sum, 5 + step, steps[step])
-
-    def sum_send(step):
-        if p.inside:
-            sum_copy(step).start()
-            bias_copy(step).start()
-
-    def sum_take(step):
-        if p.inside:
-            sum_copy(step).wait()
-            b.SUM[...] += b.SUMR[step]
-            bias_copy(step).wait()
-            b.BIA[...] += b.BIAR[step]
-
-    doubled = lax.broadcasted_iota(jnp.int32, (SUM_ROWS, 1), 0) < ROW_FFN_IN_BIAS
-    b.SUM[...] = b.SUM[...] * jnp.where(doubled, 0.5, 1.0)
-    sum_send(0)
+    grad_columns(12, R, b.O, 3 * A)
+    grad_step(13, 0)
+    grad_step(7, 2)
+    grad_step(10, 1)
 
     sum4 = enc_sum(4)
     for turn in range(4):
@@ -1006,44 +1124,49 @@
             + mm(b.V[rows, :], b.ATI[2])
         )
         pair_send(sum4, i, part)
-        if turn < 2:
+        if turn == 0:
+            grad_step(9, 2)
+            late_step(2)
             across_send(sum4, i)
+        elif turn == 1:
+            across_send(sum4, i)
+            grad_step(8, 2)
+            grad_step(10, 2)
+            grad_step(7, 3)
         else:
             own = (turn - 2) * HE
             outs.enc_grad[own : own + HE, :] = b.RES[i] + pair_take(sum4, i)
-    sum_take(0)
-    sum_send(1)
-    grad_step(3, 2)
-    grad_step(4, 1)
-    grad_step(5, 1)
-    grad_step(6, 1)
-    sum_take(1)
-    sum_send(2)
-    grad_step(3, 3)
-    grad_step(4, 2)
-    grad_step(5, 2)
-    grad_step(6, 2)
-    sum_take(2)
-    sum_send(3)
+    late_step(3)
+    early_step(3)
+    grad_step(8, 3)
+    grad_step(12, 1)
+    grad_step(13, 1)
+    grad_step(9, 3)
+    late_step(4)
+    grad_step(13, 2)
+    grad_step(11, 2)
+    late_step(5)
 
     _, dec_across, _, _, _, _, dec_got, _ = dsum5
     dec_across(1 - x).wait_send()
     dec_across(x).wait_recv()
     outs.dec_grad[...] += dec_got[x].astype(F32)
+    outs.late[...] = b.LATE[...]
+    early_step(4)
+    grad_step(12, 2)
+    grad_step(10, 3)
+    grad_step(13, 3)
     _, enc_across, _, _, _, _, enc_got, _ = sum4
     for half in range(2):
         enc_across(2 * (1 - x) + half).wait_send()
         enc_across(2 * x + half).wait_recv()
         own = half * HE
         outs.enc_grad[own : own + HE, :] += enc_got[2 * x + half].astype(F32)
-    sum_take(3)
-    sum_send(4)
     grad_step(4, 3)
-    grad_step(5, 3)
-    grad_step(6, 3)
-    sum_take(4)
+    grad_step(12, 3)
+    grad_step(11, 3)
+    early_step(5)
     outs.sums[...] = b.SUM[...]
-    outs.biases[...] = b.BIA[...]
     for copy in ag_x + ag_p + ag_f:
         copy.wait_send()
 
@@ -1054,15 +1177,15 @@
 def finish(p, counts, *refs):
     D, A, F = p.D, p.A, p.F
     n = BIG_RESULTS
-    sources, (sums, biases) = refs[:n], refs[n : n + 2]
+    sources, (sums, late) = refs[:n], refs[n : n + 2]
     targets, small, sems = refs[n + 2 : 2 * n + 2], refs[2 * n + 2 : -1], refs[-1]
     copies = [pltpu.make_async_copy(sources[k], targets[k], sems.at[k]) for k in range(n)]
     for copy in copies:
         copy.start()
     att_in_bias, att_out_bias, ffn_in_bias, ffn_out_bias, gain, shift, rms = small
+    att_in_bias[:2, :] = late[LATE_NORM_ROWS : LATE_NORM_ROWS + 2, :]
+    att_in_bias[2:, :] = sums[ROW_ATT_IN_BIAS + 2 : ROW_ATT_IN_BIAS + 6, :]
     for owner in range(4):
-        first = BIAS_ROWS * owner
-        att_in_bias[:, owner * A : (owner + 1) * A] = biases[first : first + 6, :A]
         for f in range(2):
             row = ROW_FFN_IN_BIAS + 4 * f + owner
             ffn_in_bias[f : f + 1, owner * F : (owner + 1) * F] = sums[row : row + 1, :]
@@ -1070,6 +1193,8 @@
     ffn_out_bias[...] = sums[ROW_FFN_OUT_BIAS : ROW_FFN_OUT_BIAS + 2, :]
     gain[...] = sums[ROW_GAIN : ROW_GAIN + 5, :]
     shift[...] = sums[ROW_SHIFT : ROW_SHIFT + 5, :]
+    for row, target in enumerate((att_out_bias, gain, shift)):
+        target[0:1, :] = late[row : row + 1, :]
     values = jnp.zeros((1, 128), F32)
     lane = lax.broadcasted_iota(jnp.int32, (1, 128), 1)
     for k, count in enumerate(counts):
@@ -1094,7 +1219,7 @@
         enc_grad=((p.CE, D), F32),
         dec_grad=((p.HD, D), F32),
         sums=((SUM_ROWS, D), F32),
-        biases=((4 * BIAS_ROWS, 256), F32),
+        late=((LATE_ROWS, D), F32),
         probs=((4, p.heads * p.CE, p.R), BF16),
     )
     if p.inside:
@@ -1124,19 +1249,19 @@
         scratch_shapes=[
             *p.scratch.values(),
             pltpu.SemaphoreType.DMA((p.n_sems,)),
-            pltpu.SemaphoreType.REGULAR((3 * SLOTS,)),
+            pltpu.SemaphoreType.REGULAR((3 * len(GRADS),)),
         ],
         compiler_params=pltpu.CompilerParams(
             collective_id=0, has_side_effects=True, vmem_limit_bytes=63 * 2**20
         ),
     )(*named)
     made = Outputs(*[None if place is None else results[place] for place in places])
-    sums, biases = made.sums, made.biases
+    sums, late = made.sums, made.late
     if not p.inside:
-        sums, biases = lax.psum((sums, biases), (DP, TENSOR))
+        sums, late = lax.psum((sums, late), (DP, TENSOR))
         whole = made.grads.reshape(7, D, D).astype(F32)
         parts = lax.psum_scatter(whole, DP, scatter_dimension=1, tiled=True)
-        found = {grad[:2]: parts[k] for k, grad in enumerate(GRADS)}
+        found = {grad: parts[k] for k, grad in enumerate(WHOLE)}
         att = [found[ATT, a] for a in range(3)]
         made = made._replace(
             att_in=jnp.stack([att[a][:, j * A : (j + 1) * A] for a in range(3) for j in range(3)]),
@@ -1165,7 +1290,7 @@
         in_specs=[vmem] * (BIG_RESULTS + 2),
         out_specs=[hbm] * BIG_RESULTS + [vmem] * len(small),
         scratch_shapes=[pltpu.SemaphoreType.DMA((BIG_RESULTS,))],
-    )(*large, sums, biases)
+    )(*large, sums, late)
     dec_output, enc_grad, dec_grad, att_in, att_out, ffn_in, ffn_out = done[:BIG_RESULTS]
     att_in_bias, att_out_bias, ffn_in_bias, ffn_out_bias, gain, shift, rms = done[BIG_RESULTS:]
     return (

time: 251 us -> 197 us (0.78)
  Pallas kernels: 250 us -> 196 us
    pallas_call x1, Pallas kernels: 246 us -> 192 us  [body(): pl.pallas_call(functools.partial(kernel, p, places), out_shape=made_shape...]
where the time goes in v2:
time: 197 us
  Pallas kernels  196 us (99%)
    pallas_call x1, Pallas kernels, body(): pl.pallas_call(functools.partial(kernel, p, places), out_shape=made_shape...  192 us
    pallas_call x1, Pallas kernels, body(): pl.pallas_call(functools.partial(finish, p, counts), out_shape=[jax.Shape...  4.45 us

profile of v2, /device:TPU:0, one launch (start us, length us, event | category | flops | bytes accessed | tf_op | source)
XLA Modules:
  0.0 197.0 jit_solution(16392853404843589105)
XLA Ops:
  0.7 191.7 %shard_map.254 = (bf16[64,768]{1,0:T(8,128)(2,1)}, f32[256,768]{1,0:T(8,128)}, f32[64,768]{1,0:T(8,128)}, f32[40,768]{1,0:T(8,128)}, f32[8,768]{1,0:T(8,128)}, /...) custom-call(bf16[256,768]{1,0:T(8,128)(2,1)} %refs_0_.1, ...), custom_call_target="tpu_custom_call" | custom-call | tf_op jit(solution)/shard_map/pallas_call | solution.py:1244
  192.3 4.5 %shard_map.255 = (bf16[64,768]{1,0:T(8,128)(2,1)}, f32[256,768]{1,0:T(8,128)}, f32[64,768]{1,0:T(8,128)}, f32[9,96,192]{2,1,0:T(8,128)}, f32[3,96,192]{2,1,0:T(8...) custom-call(bf16[64,768]{1,0:T(8,128)(2,1)} %get-tuple-element.37.re, ...), custom_call_target="tpu_custom_call" | custom-call | tf_op jit(solution)/shard_map/pallas_call | solution.py:1286

commit v3 on v2

--- a/solution.py
+++ b/solution.py
@@ -32,19 +32,19 @@
 ATT, FFN_IN, FFN_OUT = range(3)
 GRADS = (
     (FFN_OUT, 1, (2, 1, 4), 0, 0, 2),
-    (FFN_OUT, 1, (1, 4, 2), 0, 2, 4),
-    (FFN_IN, 1, (1, 2, 4), 1, 0, 2),
-    (FFN_IN, 1, (2, 1, 4), 1, 2, 4),
+    (FFN_OUT, 1, (1, 2, 4), 0, 2, 4),
+    (FFN_IN, 1, (2, 1, 4), 1, 0, 2),
+    (FFN_IN, 1, (1, 2, 4), 1, 2, 4),
     (ATT, 2, (2, 1, 4), 2, 0, 2),
-    (ATT, 2, (1, 2, 4), 2, 2, 4),
-    (ATT, 1, (2, 1, 4), 4, 0, 2),
-    (ATT, 1, (1, 2, 4), 4, 2, 4),
-    (FFN_OUT, 0, (1, 2, 4), 3, 0, 2),
-    (FFN_OUT, 0, (2, 1, 4), 3, 2, 4),
+    (ATT, 2, (1, 4, 2), 2, 2, 4),
+    (ATT, 1, (1, 4, 2), 4, 0, 2),
+    (ATT, 1, (2, 1, 4), 4, 2, 4),
+    (FFN_OUT, 0, (1, 4, 2), 3, 0, 2),
+    (FFN_OUT, 0, (1, 2, 4), 3, 2, 4),
     (FFN_IN, 0, (2, 1, 4), 0, 0, 2),
-    (FFN_IN, 0, (1, 4, 2), 0, 2, 4),
-    (ATT, 0, (1, 4, 2), 1, 0, 2),
-    (ATT, 0, (2, 1, 4), 1, 2, 4),
+    (FFN_IN, 0, (1, 2, 4), 0, 2, 4),
+    (ATT, 0, (1, 2, 4), 1, 0, 2),
+    (ATT, 0, (1, 2, 4), 1, 2, 4),
 )
 SLOTS = 5
 WHOLE = tuple(grad[:2] for grad in GRADS if grad[4] == 0)
@@ -166,7 +166,7 @@
         self.vmem(KT=turned, VT=turned, VT2=turned)
         self.vmem(KTD=((A, S), BF16), VTD=((A, S), BF16))
         self.vmem(QD=dec_heads, KD=dec_heads, VD=dec_heads, OD=dec_heads, UPD=dec_heads)
-        self.vmem(Q2=dec_heads, O2=dec_heads, D2=dec_heads)
+        self.vmem(Q2=dec_heads, O2=dec_heads)
         self.vmem(DK=((A, R), F32), DV=((A, R), F32))
         self.vmem(BIG=((3, heads * CE, R), BF16), PD=((heads * S, S), BF16), QS=stacked, DOS=stacked)
         self.vmem(ACT0=((R, F), BF16), GP0=((R, F), BF16), ACT1=((S, F), BF16), GP1=((S, F), BF16))
@@ -225,7 +225,7 @@
     b = SimpleNamespace(**dict(zip(p.scratch, refs[n_in + n_out : -2])))
     sems, free = refs[-2:]
     b.CNT, b.DS = b.BIG.at[1], b.BIG.at[2]
-    b.KT2, b.UP, b.E3 = b.KT, b.K2, b.E5
+    b.KT2, b.UP, b.E3, b.D2 = b.KT, b.K2, b.E5, b.Q2
     D, A, F, R, S, CE, HE, CD, HD = p.D, p.A, p.F, p.R, p.S, p.CE, p.HE, p.CD, p.HD
     heads, at = p.heads, p.at
     block_rows = 128
@@ -384,6 +384,8 @@
             turned_v[:, rows] = value.T
 
     def enc_rows(i):
+        if isinstance(i, int):
+            return slice(i * CE, (i + 1) * CE)
         return pl.ds(pl.multiple_of(i * CE, CE), CE)
 
     def dec_chunk(i):
@@ -750,10 +752,6 @@
                     where = grad_place(k, 4 * a + jj)
                     rows_own = slice(jj * p.block, (jj + 1) * p.block)
                     b.GR[slot, where, :, low:high] = value[rows_own, low - first : high - first]
-
-    def both_steps(half, step):
-        grad_step(half, step)
-        grad_step(half + 1, step)
 
     def grad_copy(k, step):
         _, _, bits, slot, low, high = GRADS[k]
@@ -834,25 +832,13 @@
                 cols = slice(owner * A, (owner + 1) * A)
                 table[first + j : first + j + 1, cols] = jnp.where(t == owner, rows[j], 0.0)
 
-    transpose_into(b.E5, S)
-    grad_columns(0, S, b.ACT1, 0)
-    both_steps(0, 0)
-    transpose_into(b.G2, S)
-    grad_columns(2, S, b.GP1, 0)
-    both_steps(2, 0)
-    ffn_in_bias(1, b.GP1)
-
-    def dec_back(i, carry):
-        mine = dec_mine(i)
-        dy = b.RESD[i] + across_take(dsum3, i)
-        dz = norm_back(3, dy, b.XH3, b.RS3, i, ROW_ATT_OUT_BIAS + 2)
-        b.RESD[i] = dz
-        gather_start(at.E4, b.E4, mine, i, dz.astype(BF16))
-        return carry
-
-    lax.fori_loop(0, 2, dec_back, 0)
-    for i in range(2):
-        gather_copy(at.E4, b.E4, dec_mine(i), i).wait()
+    def decoder_ffn_out_grad():
+        transpose_into(b.E5, S)
+        grad_columns(0, S, b.ACT1, 0)
+
+    def decoder_ffn_in_grad():
+        transpose_into(b.G2, S)
+        grad_columns(2, S, b.GP1, 0)
 
     def attention_back(up_ref, q_ref, o_ref, first, k_ref, vt_ref, p_ref, d_ref, count, span):
         def one_block(index):
@@ -875,137 +861,128 @@
         for index in range(count // block_rows):
             one_block(index)
 
-    b.UPD[...] = mm_nt(b.E4[...], b.ATO[2]).astype(BF16)
-    attention_back(b.UPD, b.Q2, b.O2, jnp.int32(0), b.K2, b.VT2, b.CNT, b.D2, S, R)
+    dsum4 = dec_sum(4)
     sum2 = enc_sum(2)
-
-    for i in range(4):
-        cols = slice(i * CE, (i + 1) * CE)
-        b.K2[cols, :] = mm_tn(b.QS[: heads * S, :], b.DS[: heads * S, cols]).astype(BF16).T
-        b.V2[cols, :] = mm_tn(b.DOS[: heads * S, :], b.CNT[:, cols]).astype(BF16).T
-
-    def memory_back(i):
+    sum3 = enc_sum(3)
+    dsum5 = dec_sum(5)
+    sum4 = enc_sum(4)
+
+    def send_two(group, first, second, part_of):
+        pair_send(group, first, part_of(first))
+        part = part_of(second)
+        across_send(group, first)
+        pair_send(group, second, part)
+        across_send(group, second)
+
+    def cross_back():
+        ffn_in_bias(1, b.GP1)
+        for i in range(2):
+            mine = dec_mine(i)
+            dy = b.RESD[i] + across_take(dsum3, i)
+            dz = norm_back(3, dy, b.XH3, b.RS3, i, ROW_ATT_OUT_BIAS + 2)
+            b.RESD[i] = dz
+            gather_start(at.E4, b.E4, mine, i, dz.astype(BF16))
+        for i in range(2):
+            gather_copy(at.E4, b.E4, dec_mine(i), i).wait()
+        b.UPD[...] = mm_nt(b.E4[...], b.ATO[2]).astype(BF16)
+        attention_back(b.UPD, b.Q2, b.O2, jnp.int32(0), b.K2, b.VT2, b.CNT, b.D2, S, R)
+        for i in range(4):
+            cols = slice(i * CE, (i + 1) * CE)
+            b.K2[cols, :] = mm_tn(b.QS[: heads * S, :], b.DS[: heads * S, cols]).astype(BF16).T
+            b.V2[cols, :] = mm_tn(b.DOS[: heads * S, :], b.CNT[:, cols]).astype(BF16).T
+        att_bias(2, b.D2, b.V2)
+
+    def memory_part(i):
         rows = slice(i * CE, (i + 1) * CE)
         return mm(b.K2[rows, :], b.ATI[7]) + mm(b.V2[rows, :], b.ATI[8])
 
-    def query_back(i):
+    def query_part(i):
         return mm(b.D2[i * CD : (i + 1) * CD, :], b.ATI[6])
 
-    dsum4 = dec_sum(4)
-    pair_send(sum2, 0, memory_back(0))
-    part = memory_back(1)
-    across_send(sum2, 0)
-    pair_send(sum2, 1, part)
-    transpose_into(b.G1, S)
-    grad_columns(4, S, b.D2, 0)
-    across_send(sum2, 1)
-    transpose_into(b.MEM, R)
-    grad_columns(4, R, b.K2, A)
-    grad_step(4, 0)
-    grad_columns(4, R, b.V2, 2 * A)
-    transpose_into(b.E4, S)
-    grad_columns(4, S, b.O2, 3 * A)
-    grad_step(5, 0)
-    grad_step(1, 1)
-    sends = [(dsum4, i, query_back) for i in (0, 1)]
-    sends += [(sum2, i, memory_back) for i in (2, 3)]
-    before = None
-    for group, i, part_of in sends:
-        if group is sum2 and i == 2:
-            grad_step(0, 1)
-        part = part_of(i)
-        if before is not None:
-            across_send(*before)
-        pair_send(group, i, part)
-        before = (group, i)
-    att_bias(2, b.D2, b.V2)
-    across_send(*before)
-
-    sum3 = enc_sum(3)
-    for copy in load_ffn(0):
-        copy.wait()
+    def cross_grad(half):
+        if half == 0:
+            transpose_into(b.G1, S)
+            grad_columns(4, S, b.D2, 0)
+            transpose_into(b.MEM, R)
+            grad_columns(4, R, b.K2, A)
+        else:
+            transpose_into(b.MEM, R)
+            grad_columns(4, R, b.V2, 2 * A)
+            transpose_into(b.E4, S)
+            grad_columns(4, S, b.O2, 3 * A)
+
+    def when(condition, *steps):
+        @pl.when(condition)
+        def _():
+            for step in steps:
+                step()
 
     def ffn_back(i, carry):
         mine = enc_mine(i)
-
-        @pl.when(i == 1)
-        def _():
-            grad_step(5, 1)
-
         dy = across_take(sum2, i)
-
-        @pl.when(i == 0)
-        def _():
-            grad_step(2, 1)
-
-        @pl.when(i >= 2)
-        def _():
-            across_start(sum3, i - 2)
-
+        when(i >= 2, lambda: across_start(sum3, i - 2))
         dz = norm_back(1, dy, b.XH1, b.RS1, i, ROW_FFN_OUT_BIAS)
         b.RES[i] = dz
         gather_start(at.E2, b.E2, mine, i, dz.astype(BF16))
-
-        @pl.when(i >= 1)
-        def _():
-            across_prepare(sum3, i - 1)
-
+        when(i >= 1, lambda: across_prepare(sum3, i - 1))
+        when(i == 0, lambda: grad_step(2, 1))
+        when(i == 1, lambda: grad_step(5, 1))
+        when(i == 2, lambda: grad_step(0, 2))
         gather_copy(at.E2, b.E2, mine, i).wait()
         rows = enc_rows(i)
         pair_send(sum3, i, feed_back(rows, b.E2[rows, :], b.GP0))
+        when(i == 1, lambda: decoder_self_grad(1), lambda: grad_step(7, 0))
+        when(i == 2, lambda: grad_step(3, 2), lambda: grad_step(4, 1))
         return carry
 
-    lax.fori_loop(0, 2, ffn_back, 0)
-    grad_step(1, 2)
-    grad_step(3, 1)
-    grad_step(0, 2)
-
-    def dec_self(i, carry):
-        mine = dec_mine(i)
-        dy = b.RESD[i] + across_take(dsum4, i)
-        dz = norm_back(2, dy, b.XH2, b.RS2, i, ROW_ATT_OUT_BIAS + 1)
-        b.RESD[i] = dz
-        gather_start(at.E3, b.E3, mine, i, dz.astype(BF16))
-        return carry
-
-    lax.fori_loop(0, 2, dec_self, 0)
-    for i in range(2):
-        gather_copy(at.E3, b.E3, dec_mine(i), i).wait()
-    b.UPD[...] = mm_nt(b.E3[...], b.ATO[1]).astype(BF16)
-    attention_back(b.UPD, b.QD, b.OD, jnp.int32(0), b.KD, b.VTD, b.PD, b.QD, S, S)
-    b.KD[...] = mm_tn(b.DS[: heads * S, :S], b.QS[: heads * S, :]).astype(BF16)
-    b.VD[...] = mm_tn(b.PD[...], b.DOS[: heads * S, :]).astype(BF16)
-
-    dsum5 = dec_sum(5)
-    for turn in range(2):
-        i = 1 - x if turn == 0 else x
+    def ffn_back_rest():
+        across_start(sum3, 2)
+        across_send(sum3, 3)
+
+    def decoder_part(i):
         rows = dec_chunk(i)
-        part = (
-            mm(b.QD[rows, :], b.ATI[3])
-            + mm(b.KD[rows, :], b.ATI[4])
-            + mm(b.VD[rows, :], b.ATI[5])
+        return (
+            mm(b.QD[rows, :], b.ATI[3]) + mm(b.KD[rows, :], b.ATI[4]) + mm(b.VD[rows, :], b.ATI[5])
         )
-        pair_send(dsum5, i, part)
-        if turn == 0:
-            across_send(dsum5, i)
+
+    def decoder_self_back():
+        for i in range(2):
+            mine = dec_mine(i)
+            dy = b.RESD[i] + across_take(dsum4, i)
+            dz = norm_back(2, dy, b.XH2, b.RS2, i, ROW_ATT_OUT_BIAS + 1)
+            b.RESD[i] = dz
+            gather_start(at.E3, b.E3, mine, i, dz.astype(BF16))
+        for i in range(2):
+            gather_copy(at.E3, b.E3, dec_mine(i), i).wait()
+        b.UPD[...] = mm_nt(b.E3[...], b.ATO[1]).astype(BF16)
+        attention_back(b.UPD, b.QD, b.OD, jnp.int32(0), b.KD, b.VTD, b.PD, b.QD, S, S)
+        b.KD[...] = mm_tn(b.DS[: heads * S, :S], b.QS[: heads * S, :]).astype(BF16)
+        b.VD[...] = mm_tn(b.PD[...], b.DOS[: heads * S, :]).astype(BF16)
+        pair_send(dsum5, 1 - x, decoder_part(1 - x))
+        part = decoder_part(x)
+        across_send(dsum5, 1 - x)
+        pair_send(dsum5, x, part)
+        att_bias(1, b.QD, b.VD)
+        outs.dec_grad[...] = b.RESD[x] + pair_take(dsum5, x)
+
+    def decoder_self_grad(half):
+        if half == 0:
+            transpose_into(b.DX, S)
+            grad_columns(6, S, b.QD, 0)
+            grad_columns(6, S, b.KD, A)
         else:
-            outs.dec_grad[...] = b.RESD[i] + pair_take(dsum5, i)
-
-    transpose_into(b.DX, S)
-    grad_columns(6, S, b.QD, 0)
-    grad_columns(6, S, b.KD, A)
-    grad_step(4, 1)
-    grad_step(6, 0)
-    grad_columns(6, S, b.VD, 2 * A)
-    transpose_into(b.E3, S)
-    grad_columns(6, S, b.OD, 3 * A)
-    grad_step(2, 2)
-    grad_step(7, 0)
-    att_bias(1, b.QD, b.VD)
-    lax.fori_loop(2, 4, ffn_back, 0)
-    across_start(sum3, 2)
-    across_send(sum3, 3)
-    grad_step(1, 3)
+            transpose_into(b.DX, S)
+            grad_columns(6, S, b.VD, 2 * A)
+            transpose_into(b.E3, S)
+            grad_columns(6, S, b.OD, 3 * A)
+
+    def encoder_ffn_out_grad():
+        transpose_into(b.E2, R)
+        grad_columns(8, R, b.ACT0, 0)
+
+    def encoder_ffn_in_grad():
+        transpose_into(b.H1, R)
+        grad_columns(10, R, b.GP0, 0)
 
     steps = [pair, across] + [(flipped(dp, bit), t) for bit in (1, 2, 4)]
 
@@ -1027,26 +1004,10 @@
     def late_step(step):
         total_step(b.LATE, b.LATR if p.inside else None, 5, step)
 
-    doubled = lax.broadcasted_iota(jnp.int32, (SUM_ROWS, 1), 0) < ROW_FFN_IN_BIAS
-    ffn_in_bias(0, b.GP0)
-    b.SUM[...] = b.SUM[...] * jnp.where(doubled, 0.5, 1.0)
-    transpose_into(b.E2, R)
-    grad_columns(8, R, b.ACT0, 0)
-    both_steps(8, 0)
-    grad_step(6, 1)
-    grad_step(0, 3)
-    transpose_into(b.H1, R)
-    grad_columns(10, R, b.GP0, 0)
-    grad_step(3, 2)
-    early_step(0)
-    both_steps(10, 0)
-    grad_step(2, 3)
-    grad_step(4, 2)
-
-    p_load(0).start()
-    p_load(1).start()
-    b.DK[...] = jnp.zeros((A, R), F32)
-    b.DV[...] = jnp.zeros((A, R), F32)
+    def early_rows():
+        ffn_in_bias(0, b.GP0)
+        doubled = lax.broadcasted_iota(jnp.int32, (SUM_ROWS, 1), 0) < ROW_FFN_IN_BIAS
+        b.SUM[...] = b.SUM[...] * jnp.where(doubled, 0.5, 1.0)
 
     def att_back(i, carry):
         mine = enc_mine(i)
@@ -1055,22 +1016,16 @@
         dz = norm_back(0, dy, b.XH0, b.RS0, i, ROW_ATT_OUT_BIAS)
         b.RES[i] = dz
         gather_start(at.E1, b.MEM, mine, i, dz.astype(BF16))
-
-        @pl.when(i == 0)
-        def _():
-            grad_step(7, 1)
-            early_step(1)
-            grad_step(5, 2)
-
-        @pl.when(i == 2)
-        def _():
-            grad_step(6, 2)
-
-        @pl.when(i == 3)
-        def _():
-            grad_step(11, 1)
-            grad_step(9, 1)
-
+        when(i == 0, lambda: early_step(0))
+        when(
+            i == 2,
+            lambda: grad_step(9, 1),
+            lambda: early_step(1),
+            lambda: grad_step(8, 0),
+            lambda: grad_step(2, 2),
+            lambda: grad_step(5, 2),
+        )
+        when(i == 3, lambda: grad_step(11, 1), lambda: grad_step(7, 1))
         gather_copy(at.E1, b.MEM, mine, i).wait()
         rows = enc_rows(i)
         b.UP[rows, :] = mm_nt(b.MEM[rows, :], b.ATO[0]).astype(BF16)
@@ -1081,92 +1036,139 @@
             cols = slice(2 * j * CE, 2 * (j + 1) * CE)
             b.DK[:, cols] += mm_tn(b.QS[...], b.DS[:, cols])
             b.DV[:, cols] += mm_tn(b.DOS[...], b.BIG[slot, :, cols])
-
-        @pl.when(i < 2)
-        def _():
-            p_load(i + 2).start()
-
+        when(i < 2, lambda: p_load(i + 2).start())
         return carry
 
-    lax.fori_loop(0, 4, att_back, 0)
-    for j in range(4):
-        cols = slice(j * CE, (j + 1) * CE)
-        b.K[cols, :] = b.DK[:, cols].astype(BF16).T
-        b.V[cols, :] = b.DV[:, cols].astype(BF16).T
-    grad_step(8, 1)
-    grad_step(3, 3)
-    att_bias(0, b.Q, b.V)
-    norm_rows = lax.broadcasted_iota(jnp.int32, (LATE_ROWS, 1), 0) < LATE_NORM_ROWS
-    b.LATE[...] = b.LATE[...] * jnp.where(norm_rows, 0.5, 1.0)
-    late_step(0)
-    grad_step(5, 3)
-    grad_step(6, 3)
-    early_step(2)
-    transpose_into(b.X, R)
-    grad_columns(12, R, b.Q, 0)
-    grad_columns(12, R, b.K, A)
-    grad_step(12, 0)
-    late_step(1)
-    grad_columns(12, R, b.V, 2 * A)
-    transpose_into(b.MEM, R)
-    grad_columns(12, R, b.O, 3 * A)
-    grad_step(13, 0)
-    grad_step(7, 2)
-    grad_step(10, 1)
-
-    sum4 = enc_sum(4)
-    for turn in range(4):
+    def att_back_rest():
+        for j in range(4):
+            cols = slice(j * CE, (j + 1) * CE)
+            b.K[cols, :] = b.DK[:, cols].astype(BF16).T
+            b.V[cols, :] = b.DV[:, cols].astype(BF16).T
+        att_bias(0, b.Q, b.V)
+        norm_rows = lax.broadcasted_iota(jnp.int32, (LATE_ROWS, 1), 0) < LATE_NORM_ROWS
+        b.LATE[...] = b.LATE[...] * jnp.where(norm_rows, 0.5, 1.0)
+
+    def encoder_self_grad(half):
+        if half == 0:
+            transpose_into(b.X, R)
+            grad_columns(12, R, b.Q, 0)
+            grad_columns(12, R, b.K, A)
+        else:
+            transpose_into(b.X, R)
+            grad_columns(12, R, b.V, 2 * A)
+            transpose_into(b.MEM, R)
+            grad_columns(12, R, b.O, 3 * A)
+
+    def encoder_part(turn):
         i = 2 * (1 - x) + turn if turn < 2 else 2 * x + turn - 2
         rows = enc_rows(i)
-        part = (
-            mm(b.Q[rows, :], b.ATI[0])
-            + mm(b.K[rows, :], b.ATI[1])
-            + mm(b.V[rows, :], b.ATI[2])
-        )
+        part = mm(b.Q[rows, :], b.ATI[0]) + mm(b.K[rows, :], b.ATI[1]) + mm(b.V[rows, :], b.ATI[2])
         pair_send(sum4, i, part)
-        if turn == 0:
-            grad_step(9, 2)
-            late_step(2)
+        if turn < 2:
             across_send(sum4, i)
-        elif turn == 1:
-            across_send(sum4, i)
-            grad_step(8, 2)
-            grad_step(10, 2)
-            grad_step(7, 3)
         else:
             own = (turn - 2) * HE
             outs.enc_grad[own : own + HE, :] = b.RES[i] + pair_take(sum4, i)
+
+    def decoder_last():
+        dsum5[1](1 - x).wait_send()
+        dsum5[1](x).wait_recv()
+        outs.dec_grad[...] += dsum5[6][x].astype(F32)
+
+    def encoder_last(half):
+        sum4[1](2 * (1 - x) + half).wait_send()
+        sum4[1](2 * x + half).wait_recv()
+        own = half * HE
+        outs.enc_grad[own : own + HE, :] += sum4[6][2 * x + half].astype(F32)
+
+    decoder_ffn_out_grad()
+    grad_step(0, 0)
+    grad_step(1, 0)
+    decoder_ffn_in_grad()
+    grad_step(3, 0)
+    grad_step(2, 0)
+    cross_back()
+    send_two(dsum4, 0, 1, query_part)
+    grad_step(1, 1)
+    grad_step(0, 1)
+    cross_grad(0)
+    grad_step(4, 0)
+    send_two(sum2, 0, 1, memory_part)
+    send_two(sum2, 2, 3, memory_part)
+    cross_grad(1)
+    grad_step(5, 0)
+    decoder_self_back()
+    decoder_self_grad(0)
+    grad_step(1, 2)
+    grad_step(6, 0)
+    grad_step(3, 1)
+    for copy in load_ffn(0):
+        copy.wait()
+    lax.fori_loop(0, 4, ffn_back, 0)
+    encoder_ffn_out_grad()
+    grad_step(9, 0)
+    ffn_back_rest()
+    grad_step(4, 2)
+    grad_step(0, 3)
+    grad_step(1, 3)
+    encoder_ffn_in_grad()
+    grad_step(11, 0)
+    grad_step(10, 0)
+    grad_step(6, 1)
+    early_rows()
+    p_load(0).start()
+    p_load(1).start()
+    b.DK[...] = jnp.zeros((A, R), F32)
+    b.DV[...] = jnp.zeros((A, R), F32)
+    lax.fori_loop(0, 4, att_back, 0)
+    att_back_rest()
+    grad_step(9, 2)
+    early_step(2)
+    grad_step(8, 1)
+    grad_step(6, 2)
+    grad_step(3, 3)
+    grad_step(2, 3)
+    encoder_self_grad(0)
+    encoder_self_grad(1)
+    grad_step(13, 0)
+    grad_step(7, 2)
+    early_step(3)
+    grad_step(5, 3)
+    grad_step(12, 0)
+    grad_step(11, 2)
+    late_step(0)
+    encoder_part(0)
+    encoder_part(1)
+    grad_step(9, 3)
+    grad_step(13, 1)
+    grad_step(7, 3)
+    late_step(1)
+    grad_step(6, 3)
+    early_step(4)
+    grad_step(10, 1)
+    grad_step(12, 1)
+    late_step(2)
+    grad_step(13, 2)
     late_step(3)
-    early_step(3)
+    grad_step(10, 2)
+    encoder_part(2)
+    encoder_part(3)
+    encoder_last(0)
+    encoder_last(1)
+    grad_step(8, 2)
+    grad_step(12, 2)
+    late_step(4)
+    decoder_last()
+    grad_step(11, 3)
+    grad_step(12, 3)
+    grad_step(13, 3)
+    grad_step(10, 3)
     grad_step(8, 3)
-    grad_step(12, 1)
-    grad_step(13, 1)
-    grad_step(9, 3)
-    late_step(4)
-    grad_step(13, 2)
-    grad_step(11, 2)
+    early_step(5)
+    grad_step(4, 3)
     late_step(5)
-
-    _, dec_across, _, _, _, _, dec_got, _ = dsum5
-    dec_across(1 - x).wait_send()
-    dec_across(x).wait_recv()
-    outs.dec_grad[...] += dec_got[x].astype(F32)
+    outs.sums[...] = b.SUM[...]
     outs.late[...] = b.LATE[...]
-    early_step(4)
-    grad_step(12, 2)
-    grad_step(10, 3)
-    grad_step(13, 3)
-    _, enc_across, _, _, _, _, enc_got, _ = sum4
-    for half in range(2):
-        enc_across(2 * (1 - x) + half).wait_send()
-        enc_across(2 * x + half).wait_recv()
-        own = half * HE
-        outs.enc_grad[own : own + HE, :] += enc_got[2 * x + half].astype(F32)
-    grad_step(4, 3)
-    grad_step(12, 3)
-    grad_step(11, 3)
-    early_step(5)
-    outs.sums[...] = b.SUM[...]
     for copy in ag_x + ag_p + ag_f:
         copy.wait_send()
 
@@ -1252,7 +1254,7 @@
             pltpu.SemaphoreType.REGULAR((3 * len(GRADS),)),
         ],
         compiler_params=pltpu.CompilerParams(
-            collective_id=0, has_side_effects=True, vmem_limit_bytes=63 * 2**20
+            collective_id=0, has_side_effects=True, vmem_limit_bytes=67_000_000
         ),
     )(*named)
     made = Outputs(*[None if place is None else results[place] for place in places])

time: 197 us -> 192 us (0.975)
  Pallas kernels: 196 us -> 191 us
    pallas_call x1, Pallas kernels: 192 us -> 186 us  [body(): pl.pallas_call(functools.partial(kernel, p, places), out_shape=made_shape...]
where the time goes in v3:
time: 192 us
  Pallas kernels  191 us (99%)
    pallas_call x1, Pallas kernels, body(): pl.pallas_call(functools.partial(kernel, p, places), out_shape=made_shape...  186 us
    pallas_call x1, Pallas kernels, body(): pl.pallas_call(functools.partial(finish, p, counts), out_shape=[jax.Shape...  4.45 us

profile of v3, /device:TPU:0, one launch (start us, length us, event | category | flops | bytes accessed | tf_op | source)
XLA Modules:
  0.0 191.7 jit_solution(4051909654060269737)
XLA Ops:
  0.7 186.4 %shard_map.254 = (bf16[64,768]{1,0:T(8,128)(2,1)}, f32[256,768]{1,0:T(8,128)}, f32[64,768]{1,0:T(8,128)}, f32[40,768]{1,0:T(8,128)}, f32[8,768]{1,0:T(8,128)}, /...) custom-call(bf16[256,768]{1,0:T(8,128)(2,1)} %refs_0_.1, ...), custom_call_target="tpu_custom_call" | custom-call | tf_op jit(solution)/shard_map/pallas_call | solution.py:1246
  187.1 4.5 %shard_map.255 = (bf16[64,768]{1,0:T(8,128)(2,1)}, f32[256,768]{1,0:T(8,128)}, f32[64,768]{1,0:T(8,128)}, f32[9,96,192]{2,1,0:T(8,128)}, f32[3,96,192]{2,1,0:T(8...) custom-call(bf16[64,768]{1,0:T(8,128)(2,1)} %get-tuple-element.37.re, ...), custom_call_target="tpu_custom_call" | custom-call | tf_op jit(solution)/shard_map/pallas_call | solution.py:1288
